TPU v7x, 256 devices: a whole 4x4x8 slice. The times are simulated.
256 devices in a mesh: row: 16 (over z_hi, x), col: 16 (over z_lo, y, core).
Axes of the slice: x: 4, y: 4, z: 8 (z_hi: 4, z_lo: 2; z = z_hi * 2 + z_lo), core: 2. Of those that a mesh axis runs over, the one named last changes fastest.
Arguments:
- pair: bfloat16 [512, 512, 128], P('row', 'col'), may hold values from -6 to 6
- pair_mask: int32 [512, 512], P('row', 'col'), may hold values 0 or 1
- proj_weight: bfloat16 [2, 128, 512], replicated, may hold values from -0.5 to 0.5
- gate_weight: bfloat16 [2, 128, 128], replicated, may hold values from -0.5 to 0.5
- out_weight: bfloat16 [2, 128, 128], replicated, may hold values from -0.5 to 0.5
- in_gain: float32 [2, 128], replicated, may hold values from 0.1 to 1.9
- in_bias: float32 [2, 128], replicated, may hold values from -3 to 3
- mid_gain: float32 [2, 128], replicated, may hold values from 0.1 to 1.9
- mid_bias: float32 [2, 128], replicated, may hold values from -3 to 3
Outputs:
- updated: bfloat16 [512, 512, 128], P('row', 'col')
All inputs are finite; a program needn't handle non-finite values. No bound on the sum of `pair_mask` on one device may be relied on, other than what follows from the above.
Results may differ from a plain program's by a relative error of at most 0.017.
Values may be sent and summed in bfloat16 or wider, within the bound.
No kernel may reach another device: no remote copies, remote signals or barrier semaphores. Data moves between devices by JAX's collectives and lax.ppermute only.
A program may use at most 128 MiB of HBM per device.

v0:
```python
import jax
import jax.numpy as jnp
from jax import lax
from jax.sharding import PartitionSpec as P


def layer_norm(values, gain, bias):
    mean = jnp.mean(values, axis=-1, keepdims=True)
    centered = values - mean
    var = jnp.mean(centered * centered, axis=-1, keepdims=True)
    return centered / jnp.sqrt(var + 1e-05) * gain + bias


def prepare(state, pair_mask, proj_w, gate_w, gain_in, bias_in):
    rows, cols, chans = state.shape
    hidden = proj_w.shape[1] // 4
    normed = layer_norm(state.astype(jnp.float32), gain_in, bias_in).astype(jnp.bfloat16)
    flat = normed.reshape(rows * cols, chans)
    proj = jnp.dot(flat, proj_w, preferred_element_type=jnp.float32).reshape(rows, cols, 4 * hidden)
    maskf = pair_mask.astype(jnp.float32)[:, :, None]
    left = (maskf * jax.nn.sigmoid(proj[:, :, :hidden]) * proj[:, :, hidden : 2 * hidden]).astype(
        jnp.bfloat16
    )
    right = (
        maskf * jax.nn.sigmoid(proj[:, :, 2 * hidden : 3 * hidden]) * proj[:, :, 3 * hidden :]
    ).astype(jnp.bfloat16)
    gate = jax.nn.sigmoid(jnp.dot(flat, gate_w, preferred_element_type=jnp.float32))
    return (left, right, gate)


def finish(state, tri, gate, out_w, gain_mid, bias_mid):
    rows, cols, chans = state.shape
    tri_normed = (
        layer_norm(tri, gain_mid, bias_mid).astype(jnp.bfloat16).reshape(rows * cols, tri.shape[2])
    )
    update = gate * jnp.dot(tri_normed, out_w, preferred_element_type=jnp.float32)
    return (state.astype(jnp.float32) + update.reshape(rows, cols, chans)).astype(jnp.bfloat16)


def outgoing_product(left, right):
    column = lax.all_gather(right, "row", axis=0, tiled=True)
    flipped = lax.psum_scatter(
        jnp.einsum("jkc,ikc->jic", column, left, preferred_element_type=jnp.float32).astype(
            jnp.bfloat16
        ),
        "col",
        scatter_dimension=0,
        tiled=True,
    ).astype(jnp.float32)
    return jnp.transpose(flipped, (1, 0, 2))


def incoming_product(left, right):
    panel = lax.all_gather(left, "col", axis=1, tiled=True)
    return lax.psum_scatter(
        jnp.einsum("kic,kjc->ijc", panel, right, preferred_element_type=jnp.float32).astype(
            jnp.bfloat16
        ),
        "row",
        scatter_dimension=0,
        tiled=True,
    ).astype(jnp.float32)


def body(
    pair, pair_mask, proj_weight, gate_weight, out_weight, in_gain, in_bias, mid_gain, mid_bias
):
    left, right, gate = prepare(
        pair, pair_mask, proj_weight[0], gate_weight[0], in_gain[0], in_bias[0]
    )
    tri = outgoing_product(left, right)
    state = finish(pair, tri, gate, out_weight[0], mid_gain[0], mid_bias[0])
    left, right, gate = prepare(
        state, pair_mask, proj_weight[1], gate_weight[1], in_gain[1], in_bias[1]
    )
    tri = incoming_product(left, right)
    return finish(state, tri, gate, out_weight[1], mid_gain[1], mid_bias[1])


def solution(mesh):
    return jax.shard_map(
        body,
        mesh=mesh,
        in_specs=(P("row", "col", None), P("row", "col"), P(), P(), P(), P(), P(), P(), P()),
        out_specs=P("row", "col", None),
        check_vma=False,
    )
```

profile of v0, /device:TPU:2, one launch (start us, length us, event | category | flops | bytes accessed | tf_op | source)
XLA Modules:
  0.0 378.7 jit_solution(5318516184148606467)
XLA Ops:
  6.5 0.0 all-gather.3.cloned.1.call-start
  6.5 1.2 convert_reduce_fusion.1
  7.7 1.3 fusion.16
  9.1 0.7 convert_element_type.60
  9.8 0.8 slice_bitcast_fusion.2
  10.5 1.3 fusion.19
  11.8 1.3 fusion.54
  13.2 1.0 fusion.36
  14.2 0.0 all-gather.3.cloned.1.call-update
  14.2 0.0 reduce-scatter.3.cloned.1.call-start
  14.3 1.4 copy.41
  15.7 77.6 %all-gather.3.cloned.1.call-done = bf16[512,32,128]{2,1,0:T(8,128)(2,1)} async-done(((bf16[32,32,128]{2,1,0:T(8,128)(2,1)}), bf16[512,32,128]{2,1,0:T(8,128)(2,1)}) %all-gather.3.cloned.1.call-update) | async-done | bytes 4194320 | tf_op jit(solution)/shard_map/all_gather | solution.py:41
  93.3 23.0 %copy.42 = bf16[512,32,128]{1,0,2:T(8,128)(2,1)} copy(bf16[512,32,128]{2,1,0:T(8,128)(2,1)} %all-gather.3.cloned.1.call-done) | data formatting | bytes 8388608 | tf_op jit(solution)/shard_map/all_gather | solution.py:41
  116.4 10.5 %convert_bitcast_fusion.1 = bf16[512,32,128]{0,1,2:T(8,128)(2,1)} fusion(bf16[32,32,128]{1,0,2:T(8,128)(2,1)S(1)} %copy.41, bf16[512,32,128]{1,0,2:T(8,128)(2,1)} %copy.42), kind=kOutput, calls=%fused_computation.1 | convolution fusion | flops 136314880 | bytes 8650752 | tf_op jit(solution)/shard_map/jkc,ikc->jic/dot_general | solution.py:43
  126.8 9.1 %copy.43 = bf16[512,32,128]{2,1,0:T(8,128)(2,1)} copy(bf16[512,32,128]{0,1,2:T(8,128)(2,1)} %convert_bitcast_fusion.1) | data formatting | bytes 8388608 | tf_op jit(solution)/shard_map/convert_element_type | solution.py:43
  136.0 0.0 copy-start.3
  136.0 0.0 copy-start.4
  136.0 0.0 copy-start.5
  136.0 0.0 copy-start.2
  136.0 0.0 copy-start
  136.0 0.0 reduce-scatter.3.cloned.1.call-update
  136.0 0.0 copy-start.1
  136.0 0.0 all-gather.5.cloned.1.call-start
  136.1 0.6 copy-done.3
  136.6 0.0 copy-done.4
  136.7 0.2 copy-done.5
  136.8 0.3 fusion.5
  137.1 68.3 %reduce-scatter.3.cloned.1.call-done = bf16[32,32,128]{2,1,0:T(8,128)(2,1)} async-done(((bf16[512,32,128]{2,1,0:T(8,128)(2,1)}), bf16[32,32,128]{2,1,0:T(8,128)(2,1)}) %reduce-scatter.3.cloned.1.call-update) | async-done | bytes 262160 | tf_op jit(solution)/shard_map/reduce_scatter | solution.py:42
  205.4 1.2 bitcast_reduce_fusion
  206.6 1.3 fusion.48
  207.9 1.3 fusion.51
  209.2 0.0 copy-done.2
  209.2 0.2 convolution_multiply_fusion.1
  209.5 0.0 copy-done
  209.5 0.2 convert_reduce_fusion
  209.7 0.4 fusion.12
  210.1 0.3 fusion.15
  210.4 0.0 copy-done.1
  210.5 0.4 fusion.52
  210.9 1.0 fusion.26
  211.9 0.0 all-gather.5.cloned.1.call-update
  211.9 0.2 reduce-scatter.5.cloned.1.call-start
  212.1 1.6 copy.45
  213.7 36.1 %all-gather.5.cloned.1.call-done = bf16[32,512,128]{2,1,0:T(8,128)(2,1)} async-done(((bf16[32,32,128]{2,1,0:T(8,128)(2,1)}), bf16[32,512,128]{2,1,0:T(8,128)(2,1)}) %all-gather.5.cloned.1.call-update) | async-done | bytes 4194320 | tf_op jit(solution)/shard_map/all_gather | solution.py:54
  249.8 8.0 %copy.46 = bf16[32,512,128]{1,0,2:T(8,128)(2,1)} copy(bf16[32,512,128]{2,1,0:T(8,128)(2,1)} %all-gather.5.cloned.1.call-done) | data formatting | bytes 8388608 | tf_op jit(solution)/shard_map/all_gather | solution.py:54
  257.8 5.4 %convert_bitcast_fusion = bf16[512,32,128]{0,1,2:T(8,128)(2,1)} fusion(bf16[32,32,128]{0,1,2:T(8,128)(2,1)S(1)} %copy.45, bf16[32,512,128]{1,0,2:T(8,128)(2,1)} %copy.46), kind=kOutput, calls=%fused_computation | convolution fusion | flops 136314880 | bytes 8650752 | tf_op jit(solution)/shard_map/kic,kjc->ijc/dot_general | solution.py:56
  263.2 9.1 %copy.47 = bf16[512,32,128]{2,1,0:T(8,128)(2,1)} copy(bf16[512,32,128]{0,1,2:T(8,128)(2,1)} %convert_bitcast_fusion) | data formatting | bytes 8388608 | tf_op jit(solution)/shard_map/convert_element_type | solution.py:56
  272.3 0.0 reduce-scatter.5.cloned.1.call-update
  272.3 0.3 fusion.2
  272.6 94.7 %reduce-scatter.5.cloned.1.call-done = bf16[32,32,128]{2,1,0:T(8,128)(2,1)} async-done(((bf16[512,32,128]{2,1,0:T(8,128)(2,1)}), bf16[32,32,128]{2,1,0:T(8,128)(2,1)}) %reduce-scatter.5.cloned.1.call-update) | async-done | bytes 262160 | tf_op jit(solution)/shard_map/reduce_scatter | solution.py:55
  367.4 1.2 convert_reduce_fusion.2
  368.6 1.3 fusion.20
  369.9 1.3 fusion.23
  371.2 0.2 convolution_multiply_fusion
  371.4 0.8 fusion.25
  (9 shorter events, 0.1 us)
Async XLA Ops:
  6.5 86.8 %all-gather.3.cloned.1.call-start = ((), (), s32[]{:S(2)}) async-start(), calls=%async_computation.2 | async-start | bytes 4456448 | tf_op jit(solution)/shard_map/all_gather | solution.py:41
  14.2 191.2 %reduce-scatter.3.cloned.1.call-start = ((), (), s32[]{:S(2)}) async-start(), calls=%async_computation.3 | async-start | bytes 4456448 | tf_op jit(solution)/shard_map/reduce_scatter | solution.py:42
  136.0 0.7 copy-start.3
  136.0 0.7 copy-start.4
  136.0 0.9 copy-start.5
  136.0 73.3 %copy-start.2 = (bf16[2,128,128]{2,1,0:T(8,128)(2,1)S(1)}, bf16[2,128,128]{2,1,0:T(8,128)(2,1)}, u32[]{:S(2)}) copy-start(bf16[2,128,128]{2,1,0:T(8,128)(2,1)} %param.13) | copy-start | bytes 196612
  136.0 73.5 %copy-start = (bf16[32,32,128]{2,1,0:T(8,128)(2,1)S(1)}, bf16[32,32,128]{2,1,0:T(8,128)(2,1)}, u32[]{:S(2)}) copy-start(bf16[32,32,128]{2,1,0:T(8,128)(2,1)} %param.9) | copy-start | bytes 786436
  136.0 74.4 %copy-start.1 = (bf16[2,128,512]{2,1,0:T(8,128)(2,1)S(1)}, bf16[2,128,512]{2,1,0:T(8,128)(2,1)}, u32[]{:S(2)}) copy-start(bf16[2,128,512]{2,1,0:T(8,128)(2,1)} %param.11) | copy-start | bytes 786436
  136.0 113.8 %all-gather.5.cloned.1.call-start = ((), (), s32[]{:S(2)}) async-start(), calls=%async_computation.4 | async-start | bytes 4456448 | tf_op jit(solution)/shard_map/all_gather | solution.py:54
  211.9 155.5 %reduce-scatter.5.cloned.1.call-start = ((), (), s32[]{:S(2)}) async-start(), calls=%async_computation.5 | async-start | bytes 4456448 | tf_op jit(solution)/shard_map/reduce_scatter | solution.py:55
Sparse Core Ops, SparseCore 0:
  14.3 78.9 all-gather.2
  136.1 69.2 reduce-scatter.2
  212.0 37.7 all-gather.4
  272.5 94.8 reduce-scatter.4
where the time goes:
time: 380 us; the launch traced here: 379 us
  waiting for transfers between devices  277 us (73%)
  local copies, waits for them, and re-layouts  53.9 us (14%)
  matrix products  18.6 us (5%)
  other arithmetic  15.8 us (4%)
  between operations  13.4 us (4%)
    reduce_scatter x1, waiting for transfers between devices, incoming_product(): lax.psum_scatter(jnp.einsum('kic,kjc->ijc', panel, right, preferred_eleme...  94.7 us
    all_gather x1, waiting for transfers between devices, outgoing_product(): column = lax.all_gather(right, 'row', axis=0, tiled=True)  77.6 us
    reduce_scatter x1, waiting for transfers between devices, outgoing_product(): lax.psum_scatter(jnp.einsum('jkc,ikc->jic', column, left, preferred_eleme...  68.3 us
    all_gather x1, waiting for transfers between devices, incoming_product(): panel = lax.all_gather(left, 'col', axis=1, tiled=True)  36.1 us
    all_gather x1, local copies, waits for them, and re-layouts, outgoing_product(): column = lax.all_gather(right, 'row', axis=0, tiled=True)  23 us
    dot_general x1, matrix products, outgoing_product(): jnp.einsum('jkc,ikc->jic', column, left, preferred_element_type=jnp.float32)  10.5 us
    convert_element_type x1, local copies, waits for them, and re-layouts, outgoing_product(): jnp.einsum('jkc,ikc->jic', column, left, preferred_element_type=jnp.float32)  9.13 us
    convert_element_type x1, local copies, waits for them, and re-layouts, incoming_product(): jnp.einsum('kic,kjc->ijc', panel, right, preferred_element_type=jnp.float32)  9.13 us
  transfers between devices with their start and end apart: 4, of which 4 were waited for; matrix products, arithmetic and copies ran while one was open for 1% of the time, Pallas kernels for 0%

commit v1 on v0

v1 whole, which is shorter than its diff:
```python
import jax
import jax.numpy as jnp
from jax import lax
from jax.experimental import pallas as pl
from jax.experimental.pallas import tpu as pltpu
from jax.sharding import Mesh
from jax.sharding import PartitionSpec as P

F32 = jnp.float32
BF16 = jnp.bfloat16
CHIPS = ("zh", "x", "zl", "y")
VMEM_LIMIT = 48 * 1024 * 1024


def dot(a, b, dims):
    return lax.dot_general(a, b, (dims, ((), ())), preferred_element_type=F32)


def sigmoid(v):
    return 0.5 * jnp.tanh(0.5 * v) + 0.5


def columns(gains, scr):
    for n, ref in enumerate(gains):
        scr[2 * n : 2 * n + 2, :] = ref[...]
    return scr[...].T


def norm_channels(v, gain, bias):
    mean = jnp.mean(v, axis=0, keepdims=True)
    centered = v - mean
    var = jnp.mean(centered * centered, axis=0, keepdims=True)
    return centered * lax.rsqrt(var + 1e-05) * gain + bias


def swap_groups(v):
    lane = lax.broadcasted_iota(jnp.int32, v[0].shape, v[0].ndim - 1)
    low = lane < 64
    even = (lane // 32) % 2 == 0
    axis = v[0].ndim - 1

    def exchange(a, b, keep, up, down):
        return jnp.where(keep, a, pltpu.roll(b, up, axis)), jnp.where(keep, pltpu.roll(a, down, axis), b)

    a0, a2 = exchange(v[0], v[2], low, 64, 64)
    a1, a3 = exchange(v[1], v[3], low, 64, 64)
    b0, b1 = exchange(a0, a1, even, 32, 96)
    b2, b3 = exchange(a2, a3, even, 32, 96)
    return [b0, b1, b2, b3]


def project(normed, w_t, mask, a, scr):
    proj = dot(w_t, normed, ((1,), (0,)))
    hid = proj.shape[0] // 4
    row = mask[a : a + 1, :]
    left = row * sigmoid(proj[:hid]) * proj[hid : 2 * hid]
    right = row * sigmoid(proj[2 * hid : 3 * hid]) * proj[3 * hid :]
    scr[pl.ds(a, hid, stride=16), :] = left
    scr[pl.ds(a + 8, hid, stride=16), :] = right


def begin_kernel(pair, mask, proj_w, ig, ib, mg, mb, sent, pair_t, normed_t, mask_out, cols, scr, gains):
    col = columns((ig, ib, mg, mb), gains)
    cols[...] = col
    m = mask[...].astype(F32)
    m8 = jnp.concatenate([m[8 * q : 8 * q + 8] for q in range(4)], axis=1)
    mask_out[...] = m8
    w_t = proj_w[0].astype(F32).T.astype(BF16)
    for a in range(8):
        block = jnp.concatenate([pair[8 * q + a] for q in range(4)], axis=0).astype(F32).T
        lanes = slice(128 * a, 128 * a + 128)
        pair_t[:, lanes] = block.astype(BF16)
        normed = norm_channels(block, col[:, 0:1], col[:, 2:3]).astype(BF16)
        normed_t[:, lanes] = normed
        project(normed, w_t, m8, a, scr)
    sent[...] = scr[...].astype(BF16)


def update(tri, state_t, normed_t, gate_wt, out_wt, gain, bias, a, mean, rstd):
    lanes = slice(128 * a, 128 * a + 128)
    chans = state_t.shape[0]
    v = tri[pl.ds(a, chans, stride=8), :]
    v = ((v - mean[a : a + 1]) * rstd[a : a + 1] * gain + bias).astype(BF16)
    gate = sigmoid(dot(gate_wt, normed_t[:, lanes], ((1,), (0,))))
    return state_t[:, lanes].astype(F32) + gate * dot(out_wt, v, ((1,), (0,)))


def statistics(got, tri):
    v = got[...].astype(F32)
    tri[...] = v
    v = v.reshape(-1, 8, 128)
    mean = jnp.mean(v, axis=0)
    centered = v - mean[None]
    return mean, lax.rsqrt(jnp.mean(centered * centered, axis=0) + 1e-05)


def middle_kernel(got, pair_t, normed_t, mask, cols, proj_w, gate_w, out_w, sent, state_out, normed_out, tri, scr):
    col = cols[...]
    w_t = proj_w[1].astype(F32).T.astype(BF16)
    gate_wt = gate_w[0].astype(F32).T.astype(BF16)
    out_wt = out_w[0].astype(F32).T.astype(BF16)
    mean, rstd = statistics(got, tri)
    m8 = mask[...]
    for a in range(8):
        lanes = slice(128 * a, 128 * a + 128)
        state = update(tri, pair_t, normed_t, gate_wt, out_wt, col[:, 4:5], col[:, 6:7], a, mean, rstd).astype(BF16)
        state_out[:, lanes] = state
        normed = norm_channels(state.astype(F32), col[:, 1:2], col[:, 3:4]).astype(BF16)
        normed_out[:, lanes] = normed
        project(normed, w_t, m8, a, scr)
    sent[...] = scr[...].astype(BF16)


def end_kernel(got, state_t, normed_t, cols, gate_w, out_w, out, tri):
    col = cols[...]
    gate_wt = gate_w[1].astype(F32).T.astype(BF16)
    out_wt = out_w[1].astype(F32).T.astype(BF16)
    mean, rstd = statistics(got, tri)
    for a in range(8):
        state = update(tri, state_t, normed_t, gate_wt, out_wt, col[:, 5:6], col[:, 7:8], a, mean, rstd).T.astype(BF16)
        for q in range(4):
            out[8 * q + a] = state[32 * q : 32 * q + 32]


def gather_groups(got, rows, left, right):
    v = got[...].astype(F32).reshape(16, 8, rows, 128)
    for h in range(2):
        lanes = slice(128 * h, 128 * h + 128)
        for q, t in enumerate(swap_groups([v[:, 4 * h + g] for g in range(4)])):
            left[:, q, :, lanes] = t[:, :8]
            if right is not None:
                right[:, q, :, lanes] = t[:, 8:]


def scatter_groups(prod, store):
    v = prod.reshape(-1, 4, 8, 256)
    for h in range(2):
        lanes = slice(128 * h, 128 * h + 128)
        for g, t in enumerate(swap_groups([v[:, q, :, lanes] for q in range(4)])):
            store(4 * h + g, t)


def outgoing_kernel(got, keep, send, left, right, chunks):
    core = lax.axis_index("core")
    gather_groups(got, 16, left, right)
    lm = left[...].reshape(512, 256).astype(BF16)
    for parity, out in ((1 - core, send), (core, keep)):
        rm = jnp.concatenate([right[2 * n + parity] for n in range(8)], axis=0).reshape(256, 256).astype(BF16)
        prod = dot(lm, rm, ((1,), (1,)))

        def store(c, t):
            chunks[:, c] = t

        scatter_groups(prod, store)
        out[...] = chunks[...].reshape(1024, 128).astype(out.dtype)


def incoming_kernel(got, other, send, left, right, far, chunks):
    core = lax.axis_index("core")
    gather_groups(got, 16, left, right)
    gather_groups(other, 16, far, None)
    rm = right[...].reshape(512, 256).astype(BF16)
    for parity, ref in ((core, left), (1 - core, far)):
        prod = dot(ref[...].reshape(512, 256).astype(BF16), rm, ((0,), (0,)))

        def store(c, t):
            chunks[:, parity, c] = t

        scatter_groups(prod, store)
    send[...] = chunks[...].reshape(1024, 128).astype(BF16)


def call(kernel, outs, scratch):
    return pl.pallas_call(
        kernel,
        out_shape=[jax.ShapeDtypeStruct(shape, dtype) for shape, dtype in outs],
        scratch_shapes=[pltpu.VMEM(shape, F32) for shape in scratch],
        compiler_params=pltpu.CompilerParams(vmem_limit_bytes=VMEM_LIMIT),
    )


def body(pair, mask, proj_w, gate_w, out_w, ig, ib, mg, mb):
    def exchange(v):
        return lax.all_to_all(v, CHIPS, 0, 0, tiled=True)

    def swap(v):
        return lax.ppermute(v, "core", [(0, 1), (1, 0)])

    sent, pair_t, normed_t, m8, cols = call(
        begin_kernel,
        [((2048, 128), BF16), ((128, 1024), BF16), ((128, 1024), BF16), ((8, 128), F32), ((128, 8), F32)],
        [(2048, 128), (8, 128)],
    )(pair, mask, proj_w, ig, ib, mg, mb)
    keep, send = call(
        outgoing_kernel,
        [((1024, 128), F32), ((1024, 128), BF16)],
        [(16, 4, 8, 256), (16, 4, 8, 256), (16, 8, 8, 128)],
    )(exchange(sent))
    got = exchange((keep + swap(send).astype(F32)).astype(BF16))
    sent, state_t, normed_t = call(
        middle_kernel,
        [((2048, 128), BF16), ((128, 1024), BF16), ((128, 1024), BF16)],
        [(1024, 128), (2048, 128)],
    )(got, pair_t, normed_t, m8, cols, proj_w, gate_w, out_w)
    got = exchange(sent)
    (send,) = call(
        incoming_kernel,
        [((1024, 128), BF16)],
        [(16, 4, 8, 256), (16, 4, 8, 256), (16, 4, 8, 256), (8, 2, 8, 8, 128)],
    )(got, swap(got))
    (out,) = call(end_kernel, [((32, 32, 128), BF16)], [(1024, 128)])(
        exchange(send), state_t, normed_t, cols, gate_w, out_w
    )
    return out


def solution(mesh):
    fine = Mesh(mesh.devices.reshape(4, 4, 2, 4, 2), ("zh", "x", "zl", "y", "core"))
    block = P(("zh", "x"), ("zl", "y", "core"))
    return jax.shard_map(
        body,
        mesh=fine,
        in_specs=(block, block, P(), P(), P(), P(), P(), P(), P()),
        out_specs=block,
        check_vma=False,
    )
```

time: 380 us -> 118 us (0.31)
  waiting for transfers between devices: 277 us -> 3.43 us
  blocking collectives: 0 us -> 102 us
  local copies, waits for them, and re-layouts: 53.9 us -> 5.35 us
  matrix products: 18.6 us -> 0 us
  other arithmetic: 15.8 us -> 0.05 us
  between operations: 13.4 us -> 0.08 us
  Pallas kernels: 0 us -> 7.07 us
    reduce_scatter x2 -> x0, waiting for transfers between devices: 163 us -> none  [the longest x1 94.7 us: incoming_product(): lax.psum_scatter(jnp.einsum('kic,kjc->ijc', panel, right, preferred_eleme...]
    all_gather x2 -> x0, waiting for transfers between devices: 114 us -> none  [the longest x1 77.6 us: outgoing_product(): column = lax.all_gather(right, 'row', axis=0, tiled=True)]
    all_to_all x0 -> x4, blocking collectives: none -> 102 us  [exchange(): return lax.all_to_all(v, CHIPS, 0, 0, tiled=True)]
    all_gather x2 -> x0, local copies, waits for them, and re-layouts: 31 us -> none  [the longest x1 23 us: outgoing_product(): column = lax.all_gather(right, 'row', axis=0, tiled=True)]
    convert_element_type x4 -> x0, local copies, waits for them, and re-layouts: 21.3 us -> none  [the longest x1 9.13 us: outgoing_product(): jnp.einsum('jkc,ikc->jic', column, left, preferred_element_type=jnp.float32)]
    dot_general x8 -> x0, matrix products: 18.6 us -> none  [the longest x1 10.5 us: outgoing_product(): jnp.einsum('jkc,ikc->jic', column, left, preferred_element_type=jnp.float32)]
    reduce_sum x8 -> x0, other arithmetic: 8.04 us -> none  [the longest x4 4.36 us: layer_norm(): var = jnp.mean(centered * centered, axis=-1, keepdims=True)]
    convert_element_type x8 -> x0, other arithmetic: 7.74 us -> none  [the longest x2 2.58 us: finish(): layer_norm(tri, gain_mid, bias_mid).astype(jnp.bfloat16)]
  transfers between devices with their start and end apart: 4 -> 2, of which waited for: 4 -> 2; matrix products, arithmetic and copies ran while one was open for 1% -> 0% of each run, Pallas kernels for 0% -> 0%
where the time goes in v1:
time: 118 us
  blocking collectives  102 us (86%)
  Pallas kernels  7.07 us (6%)
  local copies, waits for them, and re-layouts  5.35 us (5%)
  waiting for transfers between devices  3.43 us (3%)
    all_to_all x4, blocking collectives, exchange(): return lax.all_to_all(v, CHIPS, 0, 0, tiled=True)  102 us
    unnamed x20, local copies, waits for them, and re-layouts  5.35 us
    ppermute x2, waiting for transfers between devices, swap(): return lax.ppermute(v, 'core', [(0, 1), (1, 0)])  3.43 us
  transfers between devices with their start and end apart: 2, of which 2 were waited for; matrix products, arithmetic and copies ran while one was open for 0% of the time, Pallas kernels for 0%

profile of v1, /device:TPU:2, one launch (start us, length us, event | category | flops | bytes accessed | tf_op | source)
XLA Modules:
  0.0 118.1 jit_solution(7422854147514509694)
XLA Ops:
  0.0 0.0 copy-start
  0.0 0.9 copy-done
  1.0 0.0 copy-start.4
  1.0 0.9 copy-done.4
  1.9 0.0 copy-start.5
  1.9 0.7 copy-done.5
  2.6 0.0 copy-start.6
  2.6 0.7 copy-done.6
  3.3 0.0 copy-start.7
  3.3 0.7 copy-done.7
  4.0 0.0 copy-start.8
  4.0 0.7 copy-done.8
  4.7 0.0 copy-start.9
  4.7 0.7 copy-done.9
  5.3 1.1 shard_map.91
  6.4 34.6 %all_to_all.44 = bf16[128,16,128]{2,1,0:T(8,128)(2,1)S(1)} all-to-all(bf16[128,16,128]{2,1,0:T(8,128)(2,1)S(1)} %bitcast.16), channel_id=1, replica_groups=mesh['zh'=4,'x'=4,'zl'=2,'y'=4,'core'=2] {'zh','x','zl','y'}, dimensions={0} | all-to-all | bytes 1048576 | tf_op jit(solution)/shard_map/all_to_all | solution.py:184
  41.0 1.1 shard_map.92
  42.1 0.1 collective-permute-start
  42.2 1.5 %collective-permute-done = bf16[1024,128]{1,0:T(8,128)(2,1)S(1)} collective-permute-done((bf16[1024,128]{1,0:T(8,128)(2,1)S(1)}, bf16[1024,128]{1,0:T(8,128)(2,1)S(1)}, u32[]{:S(2)}, u32[]{:S(2)}) %collective-permute-start) | collective-permute-done | bytes 262176 | tf_op jit(solution)/shard_map/ppermute | solution.py:187
  43.7 0.1 fusion
  43.8 0.0 copy-start.1
  43.8 0.0 copy-start.2
  43.8 0.0 copy-start.3
  43.8 21.2 %all_to_all.45 = bf16[128,8,128]{2,1,0:T(8,128)(2,1)S(1)} all-to-all(bf16[128,8,128]{2,1,0:T(8,128)(2,1)S(1)} %fusion), channel_id=1, replica_groups=mesh['zh'=4,'x'=4,'zl'=2,'y'=4,'core'=2] {'zh','x','zl','y'}, dimensions={0} | all-to-all | bytes 524288 | tf_op jit(solution)/shard_map/all_to_all | solution.py:184
  65.0 0.0 copy-done.1
  65.0 0.0 copy-done.2
  65.0 0.0 copy-done.3
  65.0 2.0 %shard_map.93 = (bf16[2048,128]{1,0:T(8,128)(2,1)S(1)}, bf16[128,1024]{1,0:T(8,128)(2,1)S(1)}, bf16[128,1024]{1,0:T(8,128)(2,1)S(1)}) custom-call(bf16[1024,128]{1,0:T(8,128)(2,1)S(1)} %bitcast.12, bf16[128,1024]{1,0:T(8,128)(2,1)S(1)} %get-tuple-element.18.pair_t, bf16[128,1024]{1,0:T(8,128)(2,1)S(1)} %get-tuple-element.19.normed_t, ...), custom_call_target="tpu_custom_call" | custom-call | tf_op jit(solution)/shard_map/pallas_call | solution.py:200
  67.0 25.1 %all_to_all.46 = bf16[128,16,128]{2,1,0:T(8,128)(2,1)S(1)} all-to-all(bf16[128,16,128]{2,1,0:T(8,128)(2,1)S(1)} %bitcast.15), channel_id=1, replica_groups=mesh['zh'=4,'x'=4,'zl'=2,'y'=4,'core'=2] {'zh','x','zl','y'}, dimensions={0} | all-to-all | bytes 1048576 | tf_op jit(solution)/shard_map/all_to_all | solution.py:184
  92.1 0.0 collective-permute-start.1
  92.1 1.9 %collective-permute-done.1.other = bf16[2048,128]{1,0:T(8,128)(2,1)S(1)} collective-permute-done((bf16[2048,128]{1,0:T(8,128)(2,1)S(1)}, bf16[2048,128]{1,0:T(8,128)(2,1)S(1)}, u32[]{:S(2)}, u32[]{:S(2)}) %collective-permute-start.1) | collective-permute-done | bytes 524320 | tf_op jit(solution)/shard_map/ppermute | solution.py:187
  94.0 1.4 %shard_map.94 = bf16[1024,128]{1,0:T(8,128)(2,1)S(1)} custom-call(bf16[2048,128]{1,0:T(8,128)(2,1)S(1)} %bitcast.10, bf16[2048,128]{1,0:T(8,128)(2,1)S(1)} %collective-permute-done.1.other), custom_call_target="tpu_custom_call" | custom-call | tf_op jit(solution)/shard_map/pallas_call | solution.py:206
  95.4 21.2 %all_to_all.47 = bf16[128,8,128]{2,1,0:T(8,128)(2,1)S(1)} all-to-all(bf16[128,8,128]{2,1,0:T(8,128)(2,1)S(1)} %bitcast.14), channel_id=1, replica_groups=mesh['zh'=4,'x'=4,'zl'=2,'y'=4,'core'=2] {'zh','x','zl','y'}, dimensions={0} | all-to-all | bytes 524288 | tf_op jit(solution)/shard_map/all_to_all | solution.py:184
  116.6 1.4 %shard_map.95 = bf16[32,32,128]{2,1,0:T(8,128)(2,1)} custom-call(bf16[1024,128]{1,0:T(8,128)(2,1)S(1)} %bitcast.13, bf16[128,1024]{1,0:T(8,128)(2,1)S(1)} %get-tuple-element.23.state_t, bf16[128,1024]{1,0:T(8,128)(2,1)S(1)} %get-tuple-element.24.normed_t, f32[128,8]{1,0:T(8,128)S(1)} %get-tuple-element.21.cols, bf16[2,128,128]{2,1,0:T(8,128)(2,1)S(1)} %copy-done.2, ...), custom_call_target="tpu_custom_call" | custom-call | tf_op jit(solution)/shard_map/pallas_call | solution.py:211
Async XLA Ops:
  0.0 0.9 copy-start
  1.0 0.9 copy-start.4
  1.9 0.7 copy-start.5
  2.6 0.7 copy-start.6
  3.3 0.7 copy-start.7
  4.0 0.7 copy-start.8
  4.7 0.7 copy-start.9
  42.1 1.6 %collective-permute-start = (bf16[1024,128]{1,0:T(8,128)(2,1)S(1)}, bf16[1024,128]{1,0:T(8,128)(2,1)S(1)}, u32[]{:S(2)}, u32[]{:S(2)}) collective-permute-start(bf16[1024,128]{1,0:T(8,128)(2,1)S(1)} %get-tuple-element.17), channel_id=1, source_target_pairs={{0,1},{1,0},{2,3},{3,2},{4,5},{5,4},{6,7},{7,6},{8,9},{9,8},{10,11... | collective-permute-start | bytes 786440 | tf_op jit(solution)/shard_map/ppermute | solution.py:187
  43.8 21.2 %copy-start.1 = (bf16[2,128,512]{2,1,0:T(8,128)(2,1)S(1)}, bf16[2,128,512]{2,1,0:T(8,128)(2,1)}, u32[]{:S(2)}) copy-start(bf16[2,128,512]{2,1,0:T(8,128)(2,1)} %proj_w.3) | copy-start | bytes 786436
  43.8 21.2 %copy-start.2 = (bf16[2,128,128]{2,1,0:T(8,128)(2,1)S(1)}, bf16[2,128,128]{2,1,0:T(8,128)(2,1)}, u32[]{:S(2)}) copy-start(bf16[2,128,128]{2,1,0:T(8,128)(2,1)} %gate_w.3) | copy-start | bytes 196612
  43.8 21.2 %copy-start.3 = (bf16[2,128,128]{2,1,0:T(8,128)(2,1)S(1)}, bf16[2,128,128]{2,1,0:T(8,128)(2,1)}, u32[]{:S(2)}) copy-start(bf16[2,128,128]{2,1,0:T(8,128)(2,1)} %out_w.3) | copy-start | bytes 196612
  92.1 1.9 %collective-permute-start.1 = (bf16[2048,128]{1,0:T(8,128)(2,1)S(1)}, bf16[2048,128]{1,0:T(8,128)(2,1)S(1)}, u32[]{:S(2)}, u32[]{:S(2)}) collective-permute-start(bf16[2048,128]{1,0:T(8,128)(2,1)S(1)} %bitcast.9), channel_id=1, source_target_pairs={{0,1},{1,0},{2,3},{3,2},{4,5},{5,4},{6,7},{7,6},{8,9},{9,8},{10,11... | collective-permute-start | bytes 1572872 | tf_op jit(solution)/shard_map/ppermute | solution.py:187

commit v2 on v1

--- a/solution.py
+++ b/solution.py
@@ -10,6 +10,7 @@
 BF16 = jnp.bfloat16
 CHIPS = ("zh", "x", "zl", "y")
 VMEM_LIMIT = 48 * 1024 * 1024
+FIRST_LIMIT = 60 * 1024 * 1024
 
 
 def dot(a, b, dims):
@@ -59,13 +60,24 @@
     scr[pl.ds(a + 8, hid, stride=16), :] = right
 
 
-def begin_kernel(pair, mask, proj_w, ig, ib, mg, mb, sent, pair_t, normed_t, mask_out, cols, scr, gains):
-    col = columns((ig, ib, mg, mb), gains)
+def begin_kernel(*refs):
+    inputs, (sent, pair_t, normed_t, mask_out, cols) = refs[:7], refs[7:12]
+    local, scr, gains, sems = refs[12:19], refs[19], refs[20], refs[21]
+    copies = [
+        pltpu.make_async_copy(src.at[0] if n == 2 else src, dst, sems.at[n])
+        for n, (src, dst) in enumerate(zip(inputs, local))
+    ]
+    for copy in copies:
+        copy.start()
+    for copy in copies:
+        copy.wait()
+    pair, mask, proj_w = local[:3]
+    col = columns(local[3:], gains)
     cols[...] = col
     m = mask[...].astype(F32)
     m8 = jnp.concatenate([m[8 * q : 8 * q + 8] for q in range(4)], axis=1)
     mask_out[...] = m8
-    w_t = proj_w[0].astype(F32).T.astype(BF16)
+    w_t = proj_w[...].astype(F32).T.astype(BF16)
     for a in range(8):
         block = jnp.concatenate([pair[8 * q + a] for q in range(4)], axis=0).astype(F32).T
         lanes = slice(128 * a, 128 * a + 128)
@@ -186,11 +198,21 @@
     def swap(v):
         return lax.ppermute(v, "core", [(0, 1), (1, 0)])
 
-    sent, pair_t, normed_t, m8, cols = call(
+    first = (pair, mask, proj_w, ig, ib, mg, mb)
+    sent, pair_t, normed_t, m8, cols = pl.pallas_call(
         begin_kernel,
-        [((2048, 128), BF16), ((128, 1024), BF16), ((128, 1024), BF16), ((8, 128), F32), ((128, 8), F32)],
-        [(2048, 128), (8, 128)],
-    )(pair, mask, proj_w, ig, ib, mg, mb)
+        in_specs=[pl.BlockSpec(memory_space=pl.ANY)] * 7,
+        out_shape=[
+            jax.ShapeDtypeStruct((2048, 128), BF16),
+            jax.ShapeDtypeStruct((128, 1024), BF16),
+            jax.ShapeDtypeStruct((128, 1024), BF16),
+            jax.ShapeDtypeStruct((8, 128), F32),
+            jax.ShapeDtypeStruct((128, 8), F32),
+        ],
+        scratch_shapes=[pltpu.VMEM(v.shape[1:] if v is proj_w else v.shape, v.dtype) for v in first]
+        + [pltpu.VMEM((2048, 128), F32), pltpu.VMEM((8, 128), F32), pltpu.SemaphoreType.DMA((7,))],
+        compiler_params=pltpu.CompilerParams(vmem_limit_bytes=FIRST_LIMIT),
+    )(*first)
     keep, send = call(
         outgoing_kernel,
         [((1024, 128), F32), ((1024, 128), BF16)],

time: 118 us -> 116 us (0.983)
  local copies, waits for them, and re-layouts: 5.35 us -> 0.66 us
  Pallas kernels: 7.07 us -> 8.93 us
    unnamed x20 -> x14, local copies, waits for them, and re-layouts: 5.35 us -> 0.66 us
    pallas_call x1, Pallas kernels: 1.06 us -> 2.92 us  [body(): pl.pallas_call(begin_kernel, in_specs=[pl.BlockSpec(memory_space=pl.ANY)]...]
where the time goes in v2:
time: 116 us; the launch traced here: 115 us
  blocking collectives  102 us (88%)
  Pallas kernels  8.93 us (8%)
  waiting for transfers between devices  3.43 us (3%)
    all_to_all x4, blocking collectives, exchange(): return lax.all_to_all(v, CHIPS, 0, 0, tiled=True)  102 us
    ppermute x2, waiting for transfers between devices, swap(): return lax.ppermute(v, 'core', [(0, 1), (1, 0)])  3.43 us
    pallas_call x1, Pallas kernels, body(): pl.pallas_call(begin_kernel, in_specs=[pl.BlockSpec(memory_space=pl.ANY)]...  2.92 us
  transfers between devices with their start and end apart: 2, of which 2 were waited for; matrix products, arithmetic and copies ran while one was open for 0% of the time, Pallas kernels for 0%

profile of v2, /device:TPU:2, one launch (start us, length us, event | category | flops | bytes accessed | tf_op | source)
XLA Modules:
  0.0 115.4 jit_solution(14228813407677338343)
XLA Ops:
  0.0 2.9 %shard_map.91 = (bf16[2048,128]{1,0:T(8,128)(2,1)}, bf16[128,1024]{1,0:T(8,128)(2,1)}, bf16[128,1024]{1,0:T(8,128)(2,1)}, f32[8,128]{1,0:T(8,128)}, f32[128,8]{1,0:T(8,128)}) custom-call(bf16[32,32,128]{2,1,0:T(8,128)(2,1)} %refs_0_.1, s32[32,32]{1,0:T(8,128)} %refs_1_.1, bf16[2,128,512]{2,1,0:T(8,128)(2,1)} %proj_w.1, f32[2,128]{1,0:T(2,128)} %refs_3_.1, ...), custom_call_target="tpu_custom_call" | custom-call | tf_op jit(solution)/shard_map/pallas_call | solution.py:202
  2.9 34.8 %all_to_all.44 = bf16[128,16,128]{2,1,0:T(8,128)(2,1)S(1)} all-to-all(bf16[128,16,128]{2,1,0:T(8,128)(2,1)} %bitcast.16), channel_id=1, replica_groups=mesh['zh'=4,'x'=4,'zl'=2,'y'=4,'core'=2] {'zh','x','zl','y'}, dimensions={0} | all-to-all | bytes 1048576 | tf_op jit(solution)/shard_map/all_to_all | solution.py:196
  37.7 1.1 shard_map.92
  38.8 0.1 collective-permute-start
  38.9 1.5 %collective-permute-done = bf16[1024,128]{1,0:T(8,128)(2,1)S(1)} collective-permute-done((bf16[1024,128]{1,0:T(8,128)(2,1)S(1)}, bf16[1024,128]{1,0:T(8,128)(2,1)S(1)}, u32[]{:S(2)}, u32[]{:S(2)}) %collective-permute-start) | collective-permute-done | bytes 262176 | tf_op jit(solution)/shard_map/ppermute | solution.py:199
  40.5 0.0 copy-start.2
  40.5 0.0 copy-start.3
  40.5 0.0 copy-start.4
  40.5 0.0 copy-start.5
  40.5 0.1 fusion
  40.5 0.0 copy-start
  40.6 0.0 copy-start.1
  40.6 21.1 %all_to_all.45 = bf16[128,8,128]{2,1,0:T(8,128)(2,1)S(1)} all-to-all(bf16[128,8,128]{2,1,0:T(8,128)(2,1)S(1)} %fusion), channel_id=1, replica_groups=mesh['zh'=4,'x'=4,'zl'=2,'y'=4,'core'=2] {'zh','x','zl','y'}, dimensions={0} | all-to-all | bytes 524288 | tf_op jit(solution)/shard_map/all_to_all | solution.py:196
  61.7 0.0 copy-start.6
  61.7 0.0 copy-done.2
  61.7 0.0 copy-done.3
  61.7 0.0 copy-done.4
  61.7 0.0 copy-done.5
  61.7 0.0 copy-done
  61.8 0.0 copy-done.1
  61.8 0.6 copy-done.6
  62.4 2.0 %shard_map.93 = (bf16[2048,128]{1,0:T(8,128)(2,1)S(1)}, bf16[128,1024]{1,0:T(8,128)(2,1)S(1)}, bf16[128,1024]{1,0:T(8,128)(2,1)S(1)}) custom-call(bf16[1024,128]{1,0:T(8,128)(2,1)S(1)} %bitcast.12, bf16[128,1024]{1,0:T(8,128)(2,1)S(1)} %copy-done.1, bf16[128,1024]{1,0:T(8,128)(2,1)S(1)} %copy-done.2, f32[8,128]{1,0:T(8,128)S(1)} %copy-done.6, ...), custom_call_target="tpu_custom_call" | custom-call | tf_op jit(solution)/shard_map/pallas_call | solution.py:222
  64.4 25.1 %all_to_all.46 = bf16[128,16,128]{2,1,0:T(8,128)(2,1)S(1)} all-to-all(bf16[128,16,128]{2,1,0:T(8,128)(2,1)S(1)} %bitcast.15), channel_id=1, replica_groups=mesh['zh'=4,'x'=4,'zl'=2,'y'=4,'core'=2] {'zh','x','zl','y'}, dimensions={0} | all-to-all | bytes 1048576 | tf_op jit(solution)/shard_map/all_to_all | solution.py:196
  89.5 0.0 collective-permute-start.1
  89.5 1.9 %collective-permute-done.1.other = bf16[2048,128]{1,0:T(8,128)(2,1)S(1)} collective-permute-done((bf16[2048,128]{1,0:T(8,128)(2,1)S(1)}, bf16[2048,128]{1,0:T(8,128)(2,1)S(1)}, u32[]{:S(2)}, u32[]{:S(2)}) %collective-permute-start.1) | collective-permute-done | bytes 524320 | tf_op jit(solution)/shard_map/ppermute | solution.py:199
  91.4 1.4 %shard_map.94 = bf16[1024,128]{1,0:T(8,128)(2,1)S(1)} custom-call(bf16[2048,128]{1,0:T(8,128)(2,1)S(1)} %bitcast.10, bf16[2048,128]{1,0:T(8,128)(2,1)S(1)} %collective-permute-done.1.other), custom_call_target="tpu_custom_call" | custom-call | tf_op jit(solution)/shard_map/pallas_call | solution.py:228
  92.8 21.2 %all_to_all.47 = bf16[128,8,128]{2,1,0:T(8,128)(2,1)S(1)} all-to-all(bf16[128,8,128]{2,1,0:T(8,128)(2,1)S(1)} %bitcast.14), channel_id=1, replica_groups=mesh['zh'=4,'x'=4,'zl'=2,'y'=4,'core'=2] {'zh','x','zl','y'}, dimensions={0} | all-to-all | bytes 524288 | tf_op jit(solution)/shard_map/all_to_all | solution.py:196
  114.0 1.4 %shard_map.95 = bf16[32,32,128]{2,1,0:T(8,128)(2,1)} custom-call(bf16[1024,128]{1,0:T(8,128)(2,1)S(1)} %bitcast.13, bf16[128,1024]{1,0:T(8,128)(2,1)S(1)} %get-tuple-element.23.state_t, bf16[128,1024]{1,0:T(8,128)(2,1)S(1)} %get-tuple-element.24.normed_t, f32[128,8]{1,0:T(8,128)S(1)} %copy-done.5, bf16[2,128,128]{2,1,0:T(8,128)(2,1)S(1)} %copy-done.3, ...), custom_call_target="tpu_custom_call" | custom-call | tf_op jit(solution)/shard_map/pallas_call | solution.py:233
Async XLA Ops:
  38.8 1.6 %collective-permute-start = (bf16[1024,128]{1,0:T(8,128)(2,1)S(1)}, bf16[1024,128]{1,0:T(8,128)(2,1)S(1)}, u32[]{:S(2)}, u32[]{:S(2)}) collective-permute-start(bf16[1024,128]{1,0:T(8,128)(2,1)S(1)} %get-tuple-element.17), channel_id=1, source_target_pairs={{0,1},{1,0},{2,3},{3,2},{4,5},{5,4},{6,7},{7,6},{8,9},{9,8},{10,11... | collective-permute-start | bytes 786440 | tf_op jit(solution)/shard_map/ppermute | solution.py:199
  40.5 21.3 %copy-start.2 = (bf16[128,1024]{1,0:T(8,128)(2,1)S(1)}, bf16[128,1024]{1,0:T(8,128)(2,1)}, u32[]{:S(2)}) copy-start(bf16[128,1024]{1,0:T(8,128)(2,1)} %get-tuple-element.19.normed_t) | copy-start | bytes 786436
  40.5 21.3 %copy-start.3 = (bf16[2,128,128]{2,1,0:T(8,128)(2,1)S(1)}, bf16[2,128,128]{2,1,0:T(8,128)(2,1)}, u32[]{:S(2)}) copy-start(bf16[2,128,128]{2,1,0:T(8,128)(2,1)} %gate_w.3) | copy-start | bytes 196612
  40.5 21.3 %copy-start.4 = (bf16[2,128,128]{2,1,0:T(8,128)(2,1)S(1)}, bf16[2,128,128]{2,1,0:T(8,128)(2,1)}, u32[]{:S(2)}) copy-start(bf16[2,128,128]{2,1,0:T(8,128)(2,1)} %out_w.3) | copy-start | bytes 196612
  40.5 21.3 %copy-start.5 = (f32[128,8]{1,0:T(8,128)S(1)}, f32[128,8]{1,0:T(8,128)}, u32[]{:S(2)}) copy-start(f32[128,8]{1,0:T(8,128)} %get-tuple-element.21.cols) | copy-start | bytes 12292
  40.5 21.2 %copy-start = (bf16[2,128,512]{2,1,0:T(8,128)(2,1)S(1)}, bf16[2,128,512]{2,1,0:T(8,128)(2,1)}, u32[]{:S(2)}) copy-start(bf16[2,128,512]{2,1,0:T(8,128)(2,1)} %proj_w.1) | copy-start | bytes 786436
  40.6 21.2 %copy-start.1 = (bf16[128,1024]{1,0:T(8,128)(2,1)S(1)}, bf16[128,1024]{1,0:T(8,128)(2,1)}, u32[]{:S(2)}) copy-start(bf16[128,1024]{1,0:T(8,128)(2,1)} %get-tuple-element.18.pair_t) | copy-start | bytes 786436
  61.7 0.7 copy-start.6
  89.5 1.9 %collective-permute-start.1 = (bf16[2048,128]{1,0:T(8,128)(2,1)S(1)}, bf16[2048,128]{1,0:T(8,128)(2,1)S(1)}, u32[]{:S(2)}, u32[]{:S(2)}) collective-permute-start(bf16[2048,128]{1,0:T(8,128)(2,1)S(1)} %bitcast.9), channel_id=1, source_target_pairs={{0,1},{1,0},{2,3},{3,2},{4,5},{5,4},{6,7},{7,6},{8,9},{9,8},{10,11... | collective-permute-start | bytes 1572872 | tf_op jit(solution)/shard_map/ppermute | solution.py:199

commit v3 on v2

v3 whole, which is shorter than its diff:
```python
import jax
import jax.numpy as jnp
from jax import lax
from jax.experimental import pallas as pl
from jax.experimental.pallas import tpu as pltpu
from jax.sharding import Mesh
from jax.sharding import PartitionSpec as P

F32 = jnp.float32
BF16 = jnp.bfloat16
CHIPS = ("zh", "x", "zl", "y")
VMEM_LIMIT = 48 * 1024 * 1024


def dot(a, b, dims):
    return lax.dot_general(a, b, (dims, ((), ())), preferred_element_type=F32)


def sigmoid(v):
    return 0.5 * jnp.tanh(0.5 * v) + 0.5


def columns(gains, scr):
    for n, ref in enumerate(gains):
        scr[2 * n : 2 * n + 2, :] = ref[...]
    return scr[...].T


def norm_channels(v, gain, bias):
    mean = jnp.mean(v, axis=0, keepdims=True)
    centered = v - mean
    var = jnp.mean(centered * centered, axis=0, keepdims=True)
    return centered * lax.rsqrt(var + 1e-05) * gain + bias


def swap_groups(v):
    lane = lax.broadcasted_iota(jnp.int32, v[0].shape, v[0].ndim - 1)
    low = lane < 64
    even = (lane // 32) % 2 == 0
    axis = v[0].ndim - 1

    def exchange(a, b, keep, up, down):
        return jnp.where(keep, a, pltpu.roll(b, up, axis)), jnp.where(keep, pltpu.roll(a, down, axis), b)

    a0, a2 = exchange(v[0], v[2], low, 64, 64)
    a1, a3 = exchange(v[1], v[3], low, 64, 64)
    b0, b1 = exchange(a0, a1, even, 32, 96)
    b2, b3 = exchange(a2, a3, even, 32, 96)
    return [b0, b1, b2, b3]


def first_mask(mask):
    m = mask[...].astype(F32)
    return jnp.concatenate([m[8 * q : 8 * q + 8] for q in range(4)], axis=1)


def transposed(w):
    return w.astype(F32).T.astype(BF16)


def lanes_of(a):
    return slice(128 * a, 128 * a + 128)


def gated(proj, mask, scr):
    hid = proj.shape[0] // 4
    for a in range(8):
        lanes = lanes_of(a)
        row = mask[a : a + 1, :]
        left = row * sigmoid(proj[:hid, lanes]) * proj[hid : 2 * hid, lanes]
        right = row * sigmoid(proj[2 * hid : 3 * hid, lanes]) * proj[3 * hid :, lanes]
        scr[pl.ds(a, hid, stride=16), :] = left
        scr[pl.ds(a + 8, hid, stride=16), :] = right


def begin_kernel(*refs):
    inputs, (sent, pair_t, normed_t, mask_out, cols) = refs[:7], refs[7:12]
    local, (scr, gains, proj, sems) = refs[12:19], refs[19:]
    parts = [(inputs[0].at[8 * n : 8 * n + 8], local[0].at[8 * n : 8 * n + 8]) for n in range(4)]
    parts += [(inputs[2].at[0], local[2]), (inputs[1], local[1])] + list(zip(inputs[3:], local[3:]))
    copies = [pltpu.make_async_copy(src, dst, sems.at[n]) for n, (src, dst) in enumerate(parts)]
    for copy in copies:
        copy.start()
    for copy in copies:
        copy.wait()
    pair, mask, proj_w = local[:3]
    col = columns(local[3:], gains)
    cols[...] = col
    m8 = first_mask(mask)
    mask_out[...] = m8
    w_t = transposed(proj_w[...])
    for a in range(8):
        block = jnp.concatenate([pair[8 * q + a] for q in range(4)], axis=0).astype(F32).T
        pair_t[:, lanes_of(a)] = block.astype(BF16)
        normed_t[:, lanes_of(a)] = norm_channels(block, col[:, 0:1], col[:, 2:3]).astype(BF16)
    proj[...] = dot(w_t, normed_t[...], ((1,), (0,)))
    gated(proj, m8, scr)
    sent[...] = scr[...].astype(BF16)


def statistics(got, tri):
    v = got[...].astype(F32)
    tri[...] = v
    v = v.reshape(8, 16, 8, 128)
    mean = jnp.mean(jnp.mean(v, axis=1), axis=0)
    centered = v - mean[None, None]
    return mean, lax.rsqrt(jnp.mean(jnp.mean(centered * centered, axis=1), axis=0) + 1e-05)


def norm_chunks(got, tri, gain, bias, out):
    mean, rstd = statistics(got, tri)
    chans = out.shape[0]
    for a in range(8):
        v = tri[pl.ds(a, chans, stride=8), :]
        out[:, lanes_of(a)] = ((v - mean[a : a + 1]) * rstd[a : a + 1] * gain + bias).astype(BF16)


def middle_kernel(got, pair_t, gate, mask, cols, w_t, out_t, sent, state_out, normed_out, tri, scr, proj, upd, tn):
    col = cols[...]
    norm_chunks(got, tri, col[:, 4:5], col[:, 6:7], tn)
    upd[...] = dot(out_t[...], tn[...], ((1,), (0,)))
    for a in range(8):
        lanes = lanes_of(a)
        state = (pair_t[:, lanes].astype(F32) + gate[:, lanes] * upd[:, lanes]).astype(BF16)
        state_out[:, lanes] = state
        normed_out[:, lanes] = norm_channels(state.astype(F32), col[:, 1:2], col[:, 3:4]).astype(BF16)
    proj[...] = dot(w_t[...], normed_out[...], ((1,), (0,)))
    gated(proj, mask[...], scr)
    sent[...] = scr[...].astype(BF16)


def end_kernel(got, state_t, gate, cols, out_t, out, tri, upd, tn):
    col = cols[...]
    norm_chunks(got, tri, col[:, 5:6], col[:, 7:8], tn)
    upd[...] = dot(out_t[...], tn[...], ((1,), (0,)))
    for a in range(8):
        lanes = lanes_of(a)
        state = (state_t[:, lanes].astype(F32) + gate[:, lanes] * upd[:, lanes]).T.astype(BF16)
        out[:, a] = state.reshape(4, 32, 128)


def gather_groups(got, rows, left, right):
    v = got[...].astype(F32).reshape(16, 8, rows, 128)
    for h in range(2):
        lanes = slice(128 * h, 128 * h + 128)
        for q, t in enumerate(swap_groups([v[:, 4 * h + g] for g in range(4)])):
            left[:, q, :, lanes] = t[:, :8]
            if right is not None:
                right[:, q, :, lanes] = t[:, 8:]


def scatter_groups(prod, store):
    v = prod.reshape(-1, 4, 8, 256)
    for h in range(2):
        lanes = slice(128 * h, 128 * h + 128)
        for g, t in enumerate(swap_groups([v[:, q, :, lanes] for q in range(4)])):
            store(4 * h + g, t)


def outgoing_chunks(lm, rm, chunks):
    prod = dot(lm, rm, ((1,), (1,)))

    def store(c, t):
        chunks[:, c] = t

    scatter_groups(prod, store)
    return chunks[...].reshape(1024, 128)


def outgoing_send_kernel(got, send, lm, rm, left, right, chunks):
    core = lax.axis_index("core")
    gather_groups(got, 16, left, right)
    lm[...] = left[...].reshape(512, 256).astype(BF16)

    def half(parity):
        return jnp.concatenate([right[2 * n + parity] for n in range(8)], axis=0).reshape(256, 256).astype(BF16)

    rm[...] = half(core)
    send[...] = outgoing_chunks(lm[...], half(1 - core), chunks).astype(BF16)


def outgoing_keep_kernel(lm, rm, normed_t, proj_w, gate_w, out_w, keep, gate, w_t, out_t, chunks):
    keep[...] = outgoing_chunks(lm[...], rm[...], chunks)
    gate[...] = sigmoid(dot(transposed(gate_w[0]), normed_t[...], ((1,), (0,))))
    w_t[...] = transposed(proj_w[1])
    out_t[...] = transposed(out_w[0])


def incoming_chunks(left, rm, store):
    scatter_groups(dot(left[...].reshape(512, 256).astype(BF16), rm, ((0,), (0,))), store)


def incoming_near_kernel(got, normed_t, gate_w, out_w, near, rm, gate, out_t, left, right):
    gather_groups(got, 16, left, right)
    rm[...] = right[...].reshape(512, 256).astype(BF16)

    def store(c, t):
        near[:, c] = t

    incoming_chunks(left, rm[...], store)
    gate[...] = sigmoid(dot(transposed(gate_w[1]), normed_t[...], ((1,), (0,))))
    out_t[...] = transposed(out_w[1])


def incoming_far_kernel(other, rm, near, send, left, chunks):
    core = lax.axis_index("core")
    chunks[:, core] = near[...]
    gather_groups(other, 16, left, None)

    def store(c, t):
        chunks[:, 1 - core, c] = t

    incoming_chunks(left, rm[...], store)
    send[...] = chunks[...].reshape(1024, 128).astype(BF16)


def call(kernel, outs, scratch, flops=0):
    return pl.pallas_call(
        kernel,
        out_shape=[jax.ShapeDtypeStruct(shape, dtype) for shape, dtype in outs],
        scratch_shapes=[pltpu.VMEM(shape, dtype) for shape, dtype in scratch],
        compiler_params=pltpu.CompilerParams(vmem_limit_bytes=VMEM_LIMIT),
        cost_estimate=pl.CostEstimate(flops=flops, bytes_accessed=1 << 20, transcendentals=1 << 17) if flops else None,
    )


def body(pair, mask, proj_w, gate_w, out_w, ig, ib, mg, mb):
    def exchange(v):
        return lax.all_to_all(v, CHIPS, 0, 0, tiled=True)

    def swap(v):
        return lax.ppermute(v, "core", [(0, 1), (1, 0)])

    first = (pair, mask, proj_w, ig, ib, mg, mb)
    sent, pair_t, normed_t, m8, cols = pl.pallas_call(
        begin_kernel,
        in_specs=[pl.BlockSpec(memory_space=pl.ANY)] * 7,
        out_shape=[
            jax.ShapeDtypeStruct((2048, 128), BF16),
            jax.ShapeDtypeStruct((128, 1024), BF16),
            jax.ShapeDtypeStruct((128, 1024), BF16),
            jax.ShapeDtypeStruct((8, 128), F32),
            jax.ShapeDtypeStruct((128, 8), F32),
        ],
        scratch_shapes=[pltpu.VMEM(v.shape[1:] if v is proj_w else v.shape, v.dtype) for v in first]
        + [
            pltpu.VMEM((2048, 128), F32),
            pltpu.VMEM((8, 128), F32),
            pltpu.VMEM((512, 1024), F32),
            pltpu.SemaphoreType.DMA((10,)),
        ],
        compiler_params=pltpu.CompilerParams(vmem_limit_bytes=VMEM_LIMIT),
    )(*(pltpu.with_memory_space_constraint(v, pltpu.HBM) for v in first))
    wide = (128, 1024)
    square = (16, 4, 8, 256)
    send, lm, rm = call(
        outgoing_send_kernel,
        [((1024, 128), BF16), ((512, 256), BF16), ((256, 256), BF16)],
        [(square, F32), (square, F32), ((16, 8, 8, 128), F32)],
    )(exchange(sent))
    far = swap(send)
    keep, gate, w_t, out_t = call(
        outgoing_keep_kernel,
        [((1024, 128), F32), (wide, F32), ((512, 128), BF16), ((128, 128), BF16)],
        [((16, 8, 8, 128), F32)],
        1 << 28,
    )(lm, rm, normed_t, proj_w, gate_w, out_w)
    got = exchange((keep + far.astype(F32)).astype(BF16))
    sent, state_t, normed_t = call(
        middle_kernel,
        [((2048, 128), BF16), (wide, BF16), (wide, BF16)],
        [((1024, 128), F32), ((2048, 128), F32), ((512, 1024), F32), (wide, F32), (wide, BF16)],
    )(got, pair_t, gate, m8, cols, w_t, out_t)
    got = exchange(sent)
    far = swap(got)
    near, rm, gate, out_t = call(
        incoming_near_kernel,
        [((8, 8, 8, 128), F32), ((512, 256), BF16), (wide, F32), ((128, 128), BF16)],
        [(square, F32), (square, F32)],
        1 << 28,
    )(got, normed_t, gate_w, out_w)
    (send,) = call(
        incoming_far_kernel,
        [((1024, 128), BF16)],
        [(square, F32), ((8, 2, 8, 8, 128), F32)],
    )(far, rm, near)
    (out,) = call(
        end_kernel,
        [((4, 8, 32, 128), BF16)],
        [((1024, 128), F32), (wide, F32), (wide, BF16)],
    )(exchange(send), state_t, gate, cols, out_t)
    return out.reshape(32, 32, 128)


def solution(mesh):
    fine = Mesh(mesh.devices.reshape(4, 4, 2, 4, 2), ("zh", "x", "zl", "y", "core"))
    block = P(("zh", "x"), ("zl", "y", "core"))
    return jax.shard_map(
        body,
        mesh=fine,
        in_specs=(block, block, P(), P(), P(), P(), P(), P(), P()),
        out_specs=block,
        check_vma=False,
    )
```

time: 116 us -> 112 us (0.966)
  waiting for transfers between devices: 3.43 us -> 1.6 us
    ppermute x2, waiting for transfers between devices: 3.43 us -> 1.6 us  [swap(): return lax.ppermute(v, 'core', [(0, 1), (1, 0)])]
    pallas_call x4 -> x6, Pallas kernels: 6.01 us -> 6.05 us  [the longest x1 1.37 us: body(): call(middle_kernel, [((2048, 128), BF16), (wide, BF16), (wide, BF16)], [(...]
  transfers between devices with their start and end apart: 2 -> 2, of which waited for: 2 -> 2; matrix products, arithmetic and copies ran while one was open for 0% -> 0% of each run, Pallas kernels for 0% -> 2%
where the time goes in v3:
time: 112 us
  blocking collectives  102 us (91%)
  Pallas kernels  8.17 us (7%)
  waiting for transfers between devices  1.6 us (1%)
    all_to_all x4, blocking collectives, exchange(): return lax.all_to_all(v, CHIPS, 0, 0, tiled=True)  102 us
  transfers between devices with their start and end apart: 2, of which 2 were waited for; matrix products, arithmetic and copies ran while one was open for 0% of the time, Pallas kernels for 2%

profile of v3, /device:TPU:2, one launch (start us, length us, event | category | flops | bytes accessed | tf_op | source)
XLA Modules:
  0.0 111.7 jit_solution(5058814870304675344)
XLA Ops:
  0.0 2.1 %shard_map.91 = (bf16[2048,128]{1,0:T(8,128)(2,1)S(1)}, bf16[128,1024]{1,0:T(8,128)(2,1)S(1)}, bf16[128,1024]{1,0:T(8,128)(2,1)S(1)}, f32[8,128]{1,0:T(8,128)S(1)}, f32[128,8]{1,0:T(8,128)S(1)}) custom-call(bf16[32,32,128]{2,1,0:T(8,128)(2,1)} %refs_0_.1, s32[32,32]{1,0:T(8,128)} %refs_1_.1, bf16[2,128,512]{2,1,0:T(8,128)(2,1)} %proj_w.1, f32[2,128]{1,0:T(2,128)} %refs_3_.1, ...), custom_call_target="tpu_custom_call" | custom-call | tf_op jit(solution)/shard_map/pallas_call | solution.py:235
  2.1 34.6 %all_to_all.44 = bf16[128,16,128]{2,1,0:T(8,128)(2,1)S(1)} all-to-all(bf16[128,16,128]{2,1,0:T(8,128)(2,1)S(1)} %bitcast.17), channel_id=1, replica_groups=mesh['zh'=4,'x'=4,'zl'=2,'y'=4,'core'=2] {'zh','x','zl','y'}, dimensions={0} | all-to-all | bytes 1048576 | tf_op jit(solution)/shard_map/all_to_all | solution.py:229
  36.7 0.0 copy-start
  36.7 0.0 copy-start.1
  36.7 0.0 copy-start.2
  36.7 0.9 shard_map.92
  37.6 0.1 collective-permute-start
  37.7 0.0 copy-done
  37.7 0.0 copy-done.1
  37.7 0.0 copy-done.2
  37.7 0.8 shard_map.93
  38.5 0.7 collective-permute-done
  39.2 0.1 fusion
  39.2 21.0 %all_to_all.45 = bf16[128,8,128]{2,1,0:T(8,128)(2,1)S(1)} all-to-all(bf16[128,8,128]{2,1,0:T(8,128)(2,1)S(1)} %fusion), channel_id=1, replica_groups=mesh['zh'=4,'x'=4,'zl'=2,'y'=4,'core'=2] {'zh','x','zl','y'}, dimensions={0} | all-to-all | bytes 524288 | tf_op jit(solution)/shard_map/all_to_all | solution.py:229
  60.3 1.4 %shard_map.94 = (bf16[2048,128]{1,0:T(8,128)(2,1)S(1)}, bf16[128,1024]{1,0:T(8,128)(2,1)S(1)}, bf16[128,1024]{1,0:T(8,128)(2,1)S(1)}) custom-call(bf16[1024,128]{1,0:T(8,128)(2,1)S(1)} %bitcast.11, bf16[128,1024]{1,0:T(8,128)(2,1)S(1)} %get-tuple-element.30.pair_t, f32[128,1024]{1,0:T(8,128)S(1)} %get-tuple-element.31.gate, ...), custom_call_target="tpu_custom_call" | custom-call | tf_op jit(solution)/shard_map/pallas_call | solution.py:269
  61.6 25.1 %all_to_all.46 = bf16[128,16,128]{2,1,0:T(8,128)(2,1)S(1)} all-to-all(bf16[128,16,128]{2,1,0:T(8,128)(2,1)S(1)} %bitcast.16), channel_id=1, replica_groups=mesh['zh'=4,'x'=4,'zl'=2,'y'=4,'core'=2] {'zh','x','zl','y'}, dimensions={0} | all-to-all | bytes 1048576 | tf_op jit(solution)/shard_map/all_to_all | solution.py:229
  86.7 0.0 collective-permute-start.1
  86.7 1.0 shard_map.95
  87.7 0.9 collective-permute-done.1.other
  88.6 0.7 shard_map.96
  89.4 21.0 %all_to_all.47 = bf16[128,8,128]{2,1,0:T(8,128)(2,1)S(1)} all-to-all(bf16[128,8,128]{2,1,0:T(8,128)(2,1)S(1)} %bitcast.12), channel_id=1, replica_groups=mesh['zh'=4,'x'=4,'zl'=2,'y'=4,'core'=2] {'zh','x','zl','y'}, dimensions={0} | all-to-all | bytes 524288 | tf_op jit(solution)/shard_map/all_to_all | solution.py:229
  110.4 1.3 %shard_map.97 = bf16[4,8,32,128]{3,2,1,0:T(8,128)(2,1)} custom-call(bf16[1024,128]{1,0:T(8,128)(2,1)S(1)} %bitcast.13, bf16[128,1024]{1,0:T(8,128)(2,1)S(1)} %get-tuple-element.40.state_t, f32[128,1024]{1,0:T(8,128)S(1)} %get-tuple-element.41.gate, f32[128,8]{1,0:T(8,128)S(1)} %get-tuple-element.33.cols, bf16[128,128]{1,0:T(8,128)(2,1)S(1)} %get-tuple-element.42.out_t), custom_call_target="tpu_custom_call" | custom-call | tf_op jit(solution)/shard_map/pallas_call | solution.py:287
Async XLA Ops:
  36.7 1.0 copy-start
  36.7 1.0 copy-start.1
  36.7 1.0 copy-start.2
  37.6 1.6 %collective-permute-start = (bf16[1024,128]{1,0:T(8,128)(2,1)S(1)}, bf16[1024,128]{1,0:T(8,128)(2,1)S(1)}, u32[]{:S(2)}, u32[]{:S(2)}) collective-permute-start(bf16[1024,128]{1,0:T(8,128)(2,1)S(1)} %get-tuple-element.29), channel_id=1, source_target_pairs={{0,1},{1,0},{2,3},{3,2},{4,5},{5,4},{6,7},{7,6},{8,9},{9,8},{10,11... | collective-permute-start | bytes 786440 | tf_op jit(solution)/shard_map/ppermute | solution.py:232
  86.7 1.9 %collective-permute-start.1 = (bf16[2048,128]{1,0:T(8,128)(2,1)S(1)}, bf16[2048,128]{1,0:T(8,128)(2,1)S(1)}, u32[]{:S(2)}, u32[]{:S(2)}) collective-permute-start(bf16[2048,128]{1,0:T(8,128)(2,1)S(1)} %bitcast.14), channel_id=1, source_target_pairs={{0,1},{1,0},{2,3},{3,2},{4,5},{5,4},{6,7},{7,6},{8,9},{9,8},{10,11... | collective-permute-start | bytes 1572872 | tf_op jit(solution)/shard_map/ppermute | solution.py:232

commit v4 on v3

--- a/solution.py
+++ b/solution.py
@@ -58,6 +58,13 @@
     return w.astype(F32).T.astype(BF16)
 
 
+def transposed_halved(w):
+    t = w.astype(F32).T
+    hid = t.shape[0] // 4
+    row = lax.broadcasted_iota(jnp.int32, t.shape, 0)
+    return jnp.where((row // hid) % 2 == 0, 0.5 * t, t).astype(BF16)
+
+
 def lanes_of(a):
     return slice(128 * a, 128 * a + 128)
 
@@ -66,9 +73,9 @@
     hid = proj.shape[0] // 4
     for a in range(8):
         lanes = lanes_of(a)
-        row = mask[a : a + 1, :]
-        left = row * sigmoid(proj[:hid, lanes]) * proj[hid : 2 * hid, lanes]
-        right = row * sigmoid(proj[2 * hid : 3 * hid, lanes]) * proj[3 * hid :, lanes]
+        row = 0.5 * mask[a : a + 1, :]
+        left = row * proj[hid : 2 * hid, lanes] * (jnp.tanh(proj[:hid, lanes]) + 1.0)
+        right = row * proj[3 * hid :, lanes] * (jnp.tanh(proj[2 * hid : 3 * hid, lanes]) + 1.0)
         scr[pl.ds(a, hid, stride=16), :] = left
         scr[pl.ds(a + 8, hid, stride=16), :] = right
 
@@ -88,7 +95,7 @@
     cols[...] = col
     m8 = first_mask(mask)
     mask_out[...] = m8
-    w_t = transposed(proj_w[...])
+    w_t = transposed_halved(proj_w[...])
     for a in range(8):
         block = jnp.concatenate([pair[8 * q + a] for q in range(4)], axis=0).astype(F32).T
         pair_t[:, lanes_of(a)] = block.astype(BF16)
@@ -139,14 +146,11 @@
         out[:, a] = state.reshape(4, 32, 128)
 
 
-def gather_groups(got, rows, left, right):
-    v = got[...].astype(F32).reshape(16, 8, rows, 128)
+def gather_groups(v, out):
+    v = v.astype(F32)
     for h in range(2):
-        lanes = slice(128 * h, 128 * h + 128)
         for q, t in enumerate(swap_groups([v[:, 4 * h + g] for g in range(4)])):
-            left[:, q, :, lanes] = t[:, :8]
-            if right is not None:
-                right[:, q, :, lanes] = t[:, 8:]
+            out[:, q, :, 128 * h : 128 * h + 128] = t
 
 
 def scatter_groups(prod, store):
@@ -167,50 +171,50 @@
     return chunks[...].reshape(1024, 128)
 
 
-def outgoing_send_kernel(got, send, lm, rm, left, right, chunks):
-    core = lax.axis_index("core")
-    gather_groups(got, 16, left, right)
+def outgoing_right(got, parity, right):
+    gather_groups(got[:, parity].astype(F32)[:, :, 8:], right)
+    return right[...].reshape(256, 256).astype(BF16)
+
+
+def outgoing_send_kernel(got, send, lm, left, right, chunks):
+    gather_groups(got[...].astype(F32).reshape(16, 8, 16, 128)[:, :, :8], left)
     lm[...] = left[...].reshape(512, 256).astype(BF16)
-
-    def half(parity):
-        return jnp.concatenate([right[2 * n + parity] for n in range(8)], axis=0).reshape(256, 256).astype(BF16)
-
-    rm[...] = half(core)
-    send[...] = outgoing_chunks(lm[...], half(1 - core), chunks).astype(BF16)
-
-
-def outgoing_keep_kernel(lm, rm, normed_t, proj_w, gate_w, out_w, keep, gate, w_t, out_t, chunks):
-    keep[...] = outgoing_chunks(lm[...], rm[...], chunks)
+    rm = outgoing_right(got, 1 - lax.axis_index("core"), right)
+    send[...] = outgoing_chunks(lm[...], rm, chunks).astype(BF16)
+
+
+def outgoing_keep_kernel(got, lm, normed_t, proj_w, gate_w, out_w, keep, gate, w_t, out_t, right, chunks):
+    keep[...] = outgoing_chunks(lm[...], outgoing_right(got, lax.axis_index("core"), right), chunks)
     gate[...] = sigmoid(dot(transposed(gate_w[0]), normed_t[...], ((1,), (0,))))
-    w_t[...] = transposed(proj_w[1])
+    w_t[...] = transposed_halved(proj_w[1])
     out_t[...] = transposed(out_w[0])
 
 
-def incoming_chunks(left, rm, store):
-    scatter_groups(dot(left[...].reshape(512, 256).astype(BF16), rm, ((0,), (0,))), store)
-
-
-def incoming_near_kernel(got, normed_t, gate_w, out_w, near, rm, gate, out_t, left, right):
-    gather_groups(got, 16, left, right)
+def incoming_left_kernel(got, lm, left):
+    gather_groups(got[...].astype(F32).reshape(16, 8, 16, 128)[:, :, :8], left)
+    lm[...] = left[...].reshape(512, 256).astype(BF16)
+
+
+def incoming_near_kernel(got, lm, normed_t, gate_w, out_w, near, rm, gate, out_t, right):
+    gather_groups(got[...].astype(F32).reshape(16, 8, 16, 128)[:, :, 8:], right)
     rm[...] = right[...].reshape(512, 256).astype(BF16)
 
     def store(c, t):
         near[:, c] = t
 
-    incoming_chunks(left, rm[...], store)
+    scatter_groups(dot(lm[...], rm[...], ((0,), (0,))), store)
     gate[...] = sigmoid(dot(transposed(gate_w[1]), normed_t[...], ((1,), (0,))))
     out_t[...] = transposed(out_w[1])
 
 
-def incoming_far_kernel(other, rm, near, send, left, chunks):
+def incoming_far_kernel(far, rm, near, send, chunks):
     core = lax.axis_index("core")
     chunks[:, core] = near[...]
-    gather_groups(other, 16, left, None)
 
     def store(c, t):
         chunks[:, 1 - core, c] = t
 
-    incoming_chunks(left, rm[...], store)
+    scatter_groups(dot(far[...], rm[...], ((0,), (0,))), store)
     send[...] = chunks[...].reshape(1024, 128).astype(BF16)
 
 
@@ -253,37 +257,36 @@
     )(*(pltpu.with_memory_space_constraint(v, pltpu.HBM) for v in first))
     wide = (128, 1024)
     square = (16, 4, 8, 256)
-    send, lm, rm = call(
+    half = (8, 4, 8, 256)
+    got = exchange(sent).reshape(8, 2, 8, 16, 128)
+    send, lm = call(
         outgoing_send_kernel,
-        [((1024, 128), BF16), ((512, 256), BF16), ((256, 256), BF16)],
-        [(square, F32), (square, F32), ((16, 8, 8, 128), F32)],
-    )(exchange(sent))
+        [((1024, 128), BF16), ((512, 256), BF16)],
+        [(square, F32), (half, F32), ((16, 8, 8, 128), F32)],
+    )(got)
     far = swap(send)
     keep, gate, w_t, out_t = call(
         outgoing_keep_kernel,
         [((1024, 128), F32), (wide, F32), ((512, 128), BF16), ((128, 128), BF16)],
-        [((16, 8, 8, 128), F32)],
+        [(half, F32), ((16, 8, 8, 128), F32)],
         1 << 28,
-    )(lm, rm, normed_t, proj_w, gate_w, out_w)
+    )(got, lm, normed_t, proj_w, gate_w, out_w)
     got = exchange((keep + far.astype(F32)).astype(BF16))
     sent, state_t, normed_t = call(
         middle_kernel,
         [((2048, 128), BF16), (wide, BF16), (wide, BF16)],
         [((1024, 128), F32), ((2048, 128), F32), ((512, 1024), F32), (wide, F32), (wide, BF16)],
     )(got, pair_t, gate, m8, cols, w_t, out_t)
-    got = exchange(sent)
-    far = swap(got)
+    got = exchange(sent).reshape(8, 2, 8, 16, 128)
+    (lm,) = call(incoming_left_kernel, [((512, 256), BF16)], [(square, F32)])(got)
+    far = swap(lm)
     near, rm, gate, out_t = call(
         incoming_near_kernel,
         [((8, 8, 8, 128), F32), ((512, 256), BF16), (wide, F32), ((128, 128), BF16)],
-        [(square, F32), (square, F32)],
+        [(square, F32)],
         1 << 28,
-    )(got, normed_t, gate_w, out_w)
-    (send,) = call(
-        incoming_far_kernel,
-        [((1024, 128), BF16)],
-        [(square, F32), ((8, 2, 8, 8, 128), F32)],
-    )(far, rm, near)
+    )(got, lm, normed_t, gate_w, out_w)
+    (send,) = call(incoming_far_kernel, [((1024, 128), BF16)], [((8, 2, 8, 8, 128), F32)])(far, rm, near)
     (out,) = call(
         end_kernel,
         [((4, 8, 32, 128), BF16)],

time: 112 us -> 112 us (level)
  no operation moved by 1% of the time
where the time goes in v4:
time: 112 us; the launch traced here: 111 us
  blocking collectives  102 us (91%)
  Pallas kernels  8.1 us (7%)
  waiting for transfers between devices  1.24 us (1%)
    all_to_all x4, blocking collectives, exchange(): return lax.all_to_all(v, CHIPS, 0, 0, tiled=True)  102 us
  transfers between devices with their start and end apart: 2, of which 2 were waited for; matrix products, arithmetic and copies ran while one was open for 0% of the time, Pallas kernels for 2%

profile of v4, /device:TPU:2, one launch (start us, length us, event | category | flops | bytes accessed | tf_op | source)
XLA Modules:
  0.0 111.4 jit_solution(4568302751325387515)
XLA Ops:
  0.0 2.1 %shard_map.91 = (bf16[2048,128]{1,0:T(8,128)(2,1)S(1)}, bf16[128,1024]{1,0:T(8,128)(2,1)S(1)}, bf16[128,1024]{1,0:T(8,128)(2,1)S(1)}, f32[8,128]{1,0:T(8,128)S(1)}, f32[128,8]{1,0:T(8,128)S(1)}) custom-call(bf16[32,32,128]{2,1,0:T(8,128)(2,1)} %refs_0_.1, s32[32,32]{1,0:T(8,128)} %refs_1_.1, bf16[2,128,512]{2,1,0:T(8,128)(2,1)} %proj_w.1, f32[2,128]{1,0:T(2,128)} %refs_3_.1, ...), custom_call_target="tpu_custom_call" | custom-call | tf_op jit(solution)/shard_map/pallas_call | solution.py:239
  2.1 34.6 %all_to_all.40 = bf16[128,16,128]{2,1,0:T(8,128)(2,1)S(1)} all-to-all(bf16[128,16,128]{2,1,0:T(8,128)(2,1)S(1)} %bitcast.18), channel_id=1, replica_groups=mesh['zh'=4,'x'=4,'zl'=2,'y'=4,'core'=2] {'zh','x','zl','y'}, dimensions={0} | all-to-all | bytes 1048576 | tf_op jit(solution)/shard_map/all_to_all | solution.py:233
  36.7 0.0 copy-start
  36.7 0.0 copy-start.1
  36.7 0.0 copy-start.2
  36.7 0.9 shard_map.92
  37.5 0.1 collective-permute-start
  37.6 0.0 copy-done
  37.6 0.0 copy-done.1
  37.6 0.0 copy-done.2
  37.7 1.0 shard_map.93
  38.7 0.5 collective-permute-done
  39.1 0.1 fusion
  39.2 21.0 %all_to_all.41 = bf16[128,8,128]{2,1,0:T(8,128)(2,1)S(1)} all-to-all(bf16[128,8,128]{2,1,0:T(8,128)(2,1)S(1)} %fusion), channel_id=1, replica_groups=mesh['zh'=4,'x'=4,'zl'=2,'y'=4,'core'=2] {'zh','x','zl','y'}, dimensions={0} | all-to-all | bytes 524288 | tf_op jit(solution)/shard_map/all_to_all | solution.py:233
  60.2 1.3 %shard_map.94 = (bf16[2048,128]{1,0:T(8,128)(2,1)S(1)}, bf16[128,1024]{1,0:T(8,128)(2,1)S(1)}, bf16[128,1024]{1,0:T(8,128)(2,1)S(1)}) custom-call(bf16[1024,128]{1,0:T(8,128)(2,1)S(1)} %bitcast.14, bf16[128,1024]{1,0:T(8,128)(2,1)S(1)} %get-tuple-element.28.pair_t, f32[128,1024]{1,0:T(8,128)S(1)} %get-tuple-element.29.gate, ...), custom_call_target="tpu_custom_call" | custom-call | tf_op jit(solution)/shard_map/pallas_call | solution.py:275
  61.6 25.1 %all_to_all.42 = bf16[128,16,128]{2,1,0:T(8,128)(2,1)S(1)} all-to-all(bf16[128,16,128]{2,1,0:T(8,128)(2,1)S(1)} %bitcast.17), channel_id=1, replica_groups=mesh['zh'=4,'x'=4,'zl'=2,'y'=4,'core'=2] {'zh','x','zl','y'}, dimensions={0} | all-to-all | bytes 1048576 | tf_op jit(solution)/shard_map/all_to_all | solution.py:233
  86.6 0.3 shard_map.95.lm
  87.0 0.1 collective-permute-start.1
  87.1 0.8 shard_map.96
  87.8 0.8 collective-permute-done.1.far
  88.6 0.5 shard_map.97
  89.0 21.0 %all_to_all.43 = bf16[128,8,128]{2,1,0:T(8,128)(2,1)S(1)} all-to-all(bf16[128,8,128]{2,1,0:T(8,128)(2,1)S(1)} %bitcast.16), channel_id=1, replica_groups=mesh['zh'=4,'x'=4,'zl'=2,'y'=4,'core'=2] {'zh','x','zl','y'}, dimensions={0} | all-to-all | bytes 524288 | tf_op jit(solution)/shard_map/all_to_all | solution.py:233
  110.1 1.3 %shard_map.98 = bf16[4,8,32,128]{3,2,1,0:T(8,128)(2,1)} custom-call(bf16[1024,128]{1,0:T(8,128)(2,1)S(1)} %bitcast.15, bf16[128,1024]{1,0:T(8,128)(2,1)S(1)} %get-tuple-element.38.state_t, f32[128,1024]{1,0:T(8,128)S(1)} %get-tuple-element.39.gate, f32[128,8]{1,0:T(8,128)S(1)} %get-tuple-element.31.cols, bf16[128,128]{1,0:T(8,128)(2,1)S(1)} %get-tuple-element.40.out_t), custom_call_target="tpu_custom_call" | custom-call | tf_op jit(solution)/shard_map/pallas_call | solution.py:290
Async XLA Ops:
  36.7 1.0 copy-start
  36.7 1.0 copy-start.1
  36.7 1.0 copy-start.2
  37.5 1.6 %collective-permute-start = (bf16[1024,128]{1,0:T(8,128)(2,1)S(1)}, bf16[1024,128]{1,0:T(8,128)(2,1)S(1)}, u32[]{:S(2)}, u32[]{:S(2)}) collective-permute-start(bf16[1024,128]{1,0:T(8,128)(2,1)S(1)} %get-tuple-element.27), channel_id=1, source_target_pairs={{0,1},{1,0},{2,3},{3,2},{4,5},{5,4},{6,7},{7,6},{8,9},{9,8},{10,11... | collective-permute-start | bytes 786440 | tf_op jit(solution)/shard_map/ppermute | solution.py:236
  87.0 1.6 %collective-permute-start.1 = (bf16[512,256]{1,0:T(8,128)(2,1)S(1)}, bf16[512,256]{1,0:T(8,128)(2,1)S(1)}, u32[]{:S(2)}, u32[]{:S(2)}) collective-permute-start(bf16[512,256]{1,0:T(8,128)(2,1)S(1)} %shard_map.95.lm), channel_id=1, source_target_pairs={{0,1},{1,0},{2,3},{3,2},{4,5},{5,4},{6,7},{7,6},{8,9},{9,8},{10,11... | collective-permute-start | bytes 786440 | tf_op jit(solution)/shard_map/ppermute | solution.py:236

commit v5 on v4

--- a/solution.py
+++ b/solution.py
@@ -10,6 +10,8 @@
 BF16 = jnp.bfloat16
 CHIPS = ("zh", "x", "zl", "y")
 VMEM_LIMIT = 48 * 1024 * 1024
+SCR = (2048 + 16, 128)
+TRI = (1024 + 8, 128)
 
 
 def dot(a, b, dims):
@@ -102,12 +104,12 @@
         normed_t[:, lanes_of(a)] = norm_channels(block, col[:, 0:1], col[:, 2:3]).astype(BF16)
     proj[...] = dot(w_t, normed_t[...], ((1,), (0,)))
     gated(proj, m8, scr)
-    sent[...] = scr[...].astype(BF16)
+    sent[...] = scr[0:2048, :].astype(BF16)
 
 
 def statistics(got, tri):
     v = got[...].astype(F32)
-    tri[...] = v
+    tri[0:1024, :] = v
     v = v.reshape(8, 16, 8, 128)
     mean = jnp.mean(jnp.mean(v, axis=1), axis=0)
     centered = v - mean[None, None]
@@ -133,7 +135,7 @@
         normed_out[:, lanes] = norm_channels(state.astype(F32), col[:, 1:2], col[:, 3:4]).astype(BF16)
     proj[...] = dot(w_t[...], normed_out[...], ((1,), (0,)))
     gated(proj, mask[...], scr)
-    sent[...] = scr[...].astype(BF16)
+    sent[...] = scr[0:2048, :].astype(BF16)
 
 
 def end_kernel(got, state_t, gate, cols, out_t, out, tri, upd, tn):
@@ -248,7 +250,7 @@
         ],
         scratch_shapes=[pltpu.VMEM(v.shape[1:] if v is proj_w else v.shape, v.dtype) for v in first]
         + [
-            pltpu.VMEM((2048, 128), F32),
+            pltpu.VMEM(SCR, F32),
             pltpu.VMEM((8, 128), F32),
             pltpu.VMEM((512, 1024), F32),
             pltpu.SemaphoreType.DMA((10,)),
@@ -275,7 +277,7 @@
     sent, state_t, normed_t = call(
         middle_kernel,
         [((2048, 128), BF16), (wide, BF16), (wide, BF16)],
-        [((1024, 128), F32), ((2048, 128), F32), ((512, 1024), F32), (wide, F32), (wide, BF16)],
+        [(TRI, F32), (SCR, F32), ((512, 1024), F32), (wide, F32), (wide, BF16)],
     )(got, pair_t, gate, m8, cols, w_t, out_t)
     got = exchange(sent).reshape(8, 2, 8, 16, 128)
     (lm,) = call(incoming_left_kernel, [((512, 256), BF16)], [(square, F32)])(got)
@@ -290,7 +292,7 @@
     (out,) = call(
         end_kernel,
         [((4, 8, 32, 128), BF16)],
-        [((1024, 128), F32), (wide, F32), (wide, BF16)],
+        [(TRI, F32), (wide, F32), (wide, BF16)],
     )(exchange(send), state_t, gate, cols, out_t)
     return out.reshape(32, 32, 128)
 

time: 112 us -> 112 us (level)
  no operation moved by 1% of the time
where the time goes in v5:
time: 112 us; the launch traced here: 111 us
  blocking collectives  102 us (91%)
  Pallas kernels  8.09 us (7%)
  waiting for transfers between devices  1.25 us (1%)
    all_to_all x4, blocking collectives, exchange(): return lax.all_to_all(v, CHIPS, 0, 0, tiled=True)  102 us
  transfers between devices with their start and end apart: 2, of which 2 were waited for; matrix products, arithmetic and copies ran while one was open for 0% of the time, Pallas kernels for 2%

profile of v5, /device:TPU:2, one launch (start us, length us, event | category | flops | bytes accessed | tf_op | source)
XLA Modules:
  0.0 111.3 jit_solution(12458735677649950693)
XLA Ops:
  0.0 2.1 %shard_map.91 = (bf16[2048,128]{1,0:T(8,128)(2,1)S(1)}, bf16[128,1024]{1,0:T(8,128)(2,1)S(1)}, bf16[128,1024]{1,0:T(8,128)(2,1)S(1)}, f32[8,128]{1,0:T(8,128)S(1)}, f32[128,8]{1,0:T(8,128)S(1)}) custom-call(bf16[32,32,128]{2,1,0:T(8,128)(2,1)} %refs_0_.1, s32[32,32]{1,0:T(8,128)} %refs_1_.1, bf16[2,128,512]{2,1,0:T(8,128)(2,1)} %proj_w.1, f32[2,128]{1,0:T(2,128)} %refs_3_.1, ...), custom_call_target="tpu_custom_call" | custom-call | tf_op jit(solution)/shard_map/pallas_call | solution.py:241
  2.1 34.6 %all_to_all.40 = bf16[128,16,128]{2,1,0:T(8,128)(2,1)S(1)} all-to-all(bf16[128,16,128]{2,1,0:T(8,128)(2,1)S(1)} %bitcast.18), channel_id=1, replica_groups=mesh['zh'=4,'x'=4,'zl'=2,'y'=4,'core'=2] {'zh','x','zl','y'}, dimensions={0} | all-to-all | bytes 1048576 | tf_op jit(solution)/shard_map/all_to_all | solution.py:235
  36.7 0.0 copy-start
  36.7 0.0 copy-start.1
  36.7 0.0 copy-start.2
  36.7 0.9 shard_map.92
  37.5 0.1 collective-permute-start
  37.6 0.0 copy-done
  37.6 0.0 copy-done.1
  37.6 0.0 copy-done.2
  37.7 1.0 shard_map.93
  38.7 0.5 collective-permute-done
  39.1 0.1 fusion
  39.2 21.0 %all_to_all.41 = bf16[128,8,128]{2,1,0:T(8,128)(2,1)S(1)} all-to-all(bf16[128,8,128]{2,1,0:T(8,128)(2,1)S(1)} %fusion), channel_id=1, replica_groups=mesh['zh'=4,'x'=4,'zl'=2,'y'=4,'core'=2] {'zh','x','zl','y'}, dimensions={0} | all-to-all | bytes 524288 | tf_op jit(solution)/shard_map/all_to_all | solution.py:235
  60.2 1.3 %shard_map.94 = (bf16[2048,128]{1,0:T(8,128)(2,1)S(1)}, bf16[128,1024]{1,0:T(8,128)(2,1)S(1)}, bf16[128,1024]{1,0:T(8,128)(2,1)S(1)}) custom-call(bf16[1024,128]{1,0:T(8,128)(2,1)S(1)} %bitcast.14, bf16[128,1024]{1,0:T(8,128)(2,1)S(1)} %get-tuple-element.28.pair_t, f32[128,1024]{1,0:T(8,128)S(1)} %get-tuple-element.29.gate, ...), custom_call_target="tpu_custom_call" | custom-call | tf_op jit(solution)/shard_map/pallas_call | solution.py:277
  61.6 25.1 %all_to_all.42 = bf16[128,16,128]{2,1,0:T(8,128)(2,1)S(1)} all-to-all(bf16[128,16,128]{2,1,0:T(8,128)(2,1)S(1)} %bitcast.17), channel_id=1, replica_groups=mesh['zh'=4,'x'=4,'zl'=2,'y'=4,'core'=2] {'zh','x','zl','y'}, dimensions={0} | all-to-all | bytes 1048576 | tf_op jit(solution)/shard_map/all_to_all | solution.py:235
  86.6 0.3 shard_map.95.lm
  86.9 0.1 collective-permute-start.1
  87.0 0.7 shard_map.96
  87.8 0.8 collective-permute-done.1.far
  88.6 0.5 shard_map.97
  89.0 21.0 %all_to_all.43 = bf16[128,8,128]{2,1,0:T(8,128)(2,1)S(1)} all-to-all(bf16[128,8,128]{2,1,0:T(8,128)(2,1)S(1)} %bitcast.16), channel_id=1, replica_groups=mesh['zh'=4,'x'=4,'zl'=2,'y'=4,'core'=2] {'zh','x','zl','y'}, dimensions={0} | all-to-all | bytes 524288 | tf_op jit(solution)/shard_map/all_to_all | solution.py:235
  110.1 1.3 %shard_map.98 = bf16[4,8,32,128]{3,2,1,0:T(8,128)(2,1)} custom-call(bf16[1024,128]{1,0:T(8,128)(2,1)S(1)} %bitcast.15, bf16[128,1024]{1,0:T(8,128)(2,1)S(1)} %get-tuple-element.38.state_t, f32[128,1024]{1,0:T(8,128)S(1)} %get-tuple-element.39.gate, f32[128,8]{1,0:T(8,128)S(1)} %get-tuple-element.31.cols, bf16[128,128]{1,0:T(8,128)(2,1)S(1)} %get-tuple-element.40.out_t), custom_call_target="tpu_custom_call" | custom-call | tf_op jit(solution)/shard_map/pallas_call | solution.py:292
Async XLA Ops:
  36.7 1.0 copy-start
  36.7 1.0 copy-start.1
  36.7 1.0 copy-start.2
  37.5 1.6 %collective-permute-start = (bf16[1024,128]{1,0:T(8,128)(2,1)S(1)}, bf16[1024,128]{1,0:T(8,128)(2,1)S(1)}, u32[]{:S(2)}, u32[]{:S(2)}) collective-permute-start(bf16[1024,128]{1,0:T(8,128)(2,1)S(1)} %get-tuple-element.27), channel_id=1, source_target_pairs={{0,1},{1,0},{2,3},{3,2},{4,5},{5,4},{6,7},{7,6},{8,9},{9,8},{10,11... | collective-permute-start | bytes 786440 | tf_op jit(solution)/shard_map/ppermute | solution.py:238
  86.9 1.6 %collective-permute-start.1 = (bf16[512,256]{1,0:T(8,128)(2,1)S(1)}, bf16[512,256]{1,0:T(8,128)(2,1)S(1)}, u32[]{:S(2)}, u32[]{:S(2)}) collective-permute-start(bf16[512,256]{1,0:T(8,128)(2,1)S(1)} %shard_map.95.lm), channel_id=1, source_target_pairs={{0,1},{1,0},{2,3},{3,2},{4,5},{5,4},{6,7},{7,6},{8,9},{9,8},{10,11... | collective-permute-start | bytes 786440 | tf_op jit(solution)/shard_map/ppermute | solution.py:238

commit v6 on v5

--- a/solution.py
+++ b/solution.py
@@ -185,11 +185,30 @@
     send[...] = outgoing_chunks(lm[...], rm, chunks).astype(BF16)
 
 
+def outgoing_own(got, lm, right, chunks):
+    return outgoing_chunks(lm[...], outgoing_right(got, lax.axis_index("core"), right), chunks)
+
+
 def outgoing_keep_kernel(got, lm, normed_t, proj_w, gate_w, out_w, keep, gate, w_t, out_t, right, chunks):
-    keep[...] = outgoing_chunks(lm[...], outgoing_right(got, lax.axis_index("core"), right), chunks)
     gate[...] = sigmoid(dot(transposed(gate_w[0]), normed_t[...], ((1,), (0,))))
     w_t[...] = transposed_halved(proj_w[1])
     out_t[...] = transposed(out_w[0])
+
+    @pl.when(lax.axis_index("core") == 1)
+    def _():
+        keep[...] = outgoing_own(got, lm, right, chunks)
+
+
+def outgoing_sum_kernel(got, lm, keep, far, total, right, chunks):
+    core = lax.axis_index("core")
+
+    @pl.when(core == 0)
+    def _():
+        total[...] = (outgoing_own(got, lm, right, chunks) + far[...].astype(F32)).astype(BF16)
+
+    @pl.when(core == 1)
+    def _():
+        total[...] = (keep[...] + far[...].astype(F32)).astype(BF16)
 
 
 def incoming_left_kernel(got, lm, left):
@@ -273,7 +292,12 @@
         [(half, F32), ((16, 8, 8, 128), F32)],
         1 << 28,
     )(got, lm, normed_t, proj_w, gate_w, out_w)
-    got = exchange((keep + far.astype(F32)).astype(BF16))
+    (total,) = call(
+        outgoing_sum_kernel,
+        [((1024, 128), BF16)],
+        [(half, F32), ((16, 8, 8, 128), F32)],
+    )(got, lm, keep, far)
+    got = exchange(total)
     sent, state_t, normed_t = call(
         middle_kernel,
         [((2048, 128), BF16), (wide, BF16), (wide, BF16)],

time: 112 us -> 111 us (level)
  blocking collectives: 102 us -> 100 us
    all_to_all x4, blocking collectives: 102 us -> 100 us  [exchange(): return lax.all_to_all(v, CHIPS, 0, 0, tiled=True)]
  transfers between devices with their start and end apart: 2 -> 2, of which waited for: 2 -> 2; matrix products, arithmetic and copies ran while one was open for 0% -> 0% of each run, Pallas kernels for 2% -> 1%
where the time goes in v6:
time: 111 us
  blocking collectives  100 us (90%)
  Pallas kernels  8.1 us (7%)
  waiting for transfers between devices  1.96 us (2%)
    all_to_all x4, blocking collectives, exchange(): return lax.all_to_all(v, CHIPS, 0, 0, tiled=True)  100 us
  transfers between devices with their start and end apart: 2, of which 2 were waited for; matrix products, arithmetic and copies ran while one was open for 0% of the time, Pallas kernels for 1%

profile of v6, /device:TPU:2, one launch (start us, length us, event | category | flops | bytes accessed | tf_op | source)
XLA Modules:
  0.0 111.0 jit_solution(13651516404353748630)
XLA Ops:
  0.0 2.1 %shard_map.91 = (bf16[2048,128]{1,0:T(8,128)(2,1)S(1)}, bf16[128,1024]{1,0:T(8,128)(2,1)S(1)}, bf16[128,1024]{1,0:T(8,128)(2,1)S(1)}, f32[8,128]{1,0:T(8,128)S(1)}, f32[128,8]{1,0:T(8,128)S(1)}) custom-call(bf16[32,32,128]{2,1,0:T(8,128)(2,1)} %refs_0_.1, s32[32,32]{1,0:T(8,128)} %refs_1_.1, bf16[2,128,512]{2,1,0:T(8,128)(2,1)} %proj_w.1, f32[2,128]{1,0:T(2,128)} %refs_3_.1, ...), custom_call_target="tpu_custom_call" | custom-call | tf_op jit(solution)/shard_map/pallas_call | solution.py:260
  2.1 34.6 %all_to_all.40 = bf16[128,16,128]{2,1,0:T(8,128)(2,1)S(1)} all-to-all(bf16[128,16,128]{2,1,0:T(8,128)(2,1)S(1)} %bitcast.19), channel_id=1, replica_groups=mesh['zh'=4,'x'=4,'zl'=2,'y'=4,'core'=2] {'zh','x','zl','y'}, dimensions={0} | all-to-all | bytes 1048576 | tf_op jit(solution)/shard_map/all_to_all | solution.py:254
  36.7 0.0 copy-start
  36.7 0.0 copy-start.1
  36.7 0.0 copy-start.2
  36.7 0.9 shard_map.92
  37.5 0.1 collective-permute-start
  37.6 0.0 copy-done
  37.6 0.0 copy-done.1
  37.6 0.0 copy-done.2
  37.7 0.3 shard_map.93
  37.9 1.2 %collective-permute-done.far = bf16[1024,128]{1,0:T(8,128)(2,1)S(1)} collective-permute-done((bf16[1024,128]{1,0:T(8,128)(2,1)S(1)}, bf16[1024,128]{1,0:T(8,128)(2,1)S(1)}, u32[]{:S(2)}, u32[]{:S(2)}) %collective-permute-start) | collective-permute-done | bytes 262176 | tf_op jit(solution)/shard_map/ppermute | solution.py:257
  39.1 0.7 shard_map.94
  39.9 20.3 %all_to_all.41 = bf16[128,8,128]{2,1,0:T(8,128)(2,1)S(1)} all-to-all(bf16[128,8,128]{2,1,0:T(8,128)(2,1)S(1)} %bitcast.15), channel_id=1, replica_groups=mesh['zh'=4,'x'=4,'zl'=2,'y'=4,'core'=2] {'zh','x','zl','y'}, dimensions={0} | all-to-all | bytes 524288 | tf_op jit(solution)/shard_map/all_to_all | solution.py:254
  60.2 1.3 %shard_map.95 = (bf16[2048,128]{1,0:T(8,128)(2,1)S(1)}, bf16[128,1024]{1,0:T(8,128)(2,1)S(1)}, bf16[128,1024]{1,0:T(8,128)(2,1)S(1)}) custom-call(bf16[1024,128]{1,0:T(8,128)(2,1)S(1)} %bitcast.14, bf16[128,1024]{1,0:T(8,128)(2,1)S(1)} %get-tuple-element.28.pair_t, f32[128,1024]{1,0:T(8,128)S(1)} %get-tuple-element.29.gate, ...), custom_call_target="tpu_custom_call" | custom-call | tf_op jit(solution)/shard_map/pallas_call | solution.py:301
  61.6 24.5 %all_to_all.42 = bf16[128,16,128]{2,1,0:T(8,128)(2,1)S(1)} all-to-all(bf16[128,16,128]{2,1,0:T(8,128)(2,1)S(1)} %bitcast.18), channel_id=1, replica_groups=mesh['zh'=4,'x'=4,'zl'=2,'y'=4,'core'=2] {'zh','x','zl','y'}, dimensions={0} | all-to-all | bytes 1048576 | tf_op jit(solution)/shard_map/all_to_all | solution.py:254
  86.1 0.3 shard_map.96.lm
  86.4 0.3 collective-permute-start.1
  86.7 0.7 shard_map.97
  87.4 0.8 collective-permute-done.1.far
  88.2 0.5 shard_map.98
  88.7 21.0 %all_to_all.43 = bf16[128,8,128]{2,1,0:T(8,128)(2,1)S(1)} all-to-all(bf16[128,8,128]{2,1,0:T(8,128)(2,1)S(1)} %bitcast.17), channel_id=1, replica_groups=mesh['zh'=4,'x'=4,'zl'=2,'y'=4,'core'=2] {'zh','x','zl','y'}, dimensions={0} | all-to-all | bytes 524288 | tf_op jit(solution)/shard_map/all_to_all | solution.py:254
  109.7 1.3 %shard_map.99 = bf16[4,8,32,128]{3,2,1,0:T(8,128)(2,1)} custom-call(bf16[1024,128]{1,0:T(8,128)(2,1)S(1)} %bitcast.16, bf16[128,1024]{1,0:T(8,128)(2,1)S(1)} %get-tuple-element.38.state_t, f32[128,1024]{1,0:T(8,128)S(1)} %get-tuple-element.39.gate, f32[128,8]{1,0:T(8,128)S(1)} %get-tuple-element.31.cols, bf16[128,128]{1,0:T(8,128)(2,1)S(1)} %get-tuple-element.40.out_t), custom_call_target="tpu_custom_call" | custom-call | tf_op jit(solution)/shard_map/pallas_call | solution.py:316
Async XLA Ops:
  36.7 1.0 copy-start
  36.7 1.0 copy-start.1
  36.7 1.0 copy-start.2
  37.5 1.6 %collective-permute-start = (bf16[1024,128]{1,0:T(8,128)(2,1)S(1)}, bf16[1024,128]{1,0:T(8,128)(2,1)S(1)}, u32[]{:S(2)}, u32[]{:S(2)}) collective-permute-start(bf16[1024,128]{1,0:T(8,128)(2,1)S(1)} %get-tuple-element.27), channel_id=1, source_target_pairs={{0,1},{1,0},{2,3},{3,2},{4,5},{5,4},{6,7},{7,6},{8,9},{9,8},{10,11... | collective-permute-start | bytes 786440 | tf_op jit(solution)/shard_map/ppermute | solution.py:257
  86.4 1.8 %collective-permute-start.1 = (bf16[512,256]{1,0:T(8,128)(2,1)S(1)}, bf16[512,256]{1,0:T(8,128)(2,1)S(1)}, u32[]{:S(2)}, u32[]{:S(2)}) collective-permute-start(bf16[512,256]{1,0:T(8,128)(2,1)S(1)} %shard_map.96.lm), channel_id=1, source_target_pairs={{0,1},{1,0},{2,3},{3,2},{4,5},{5,4},{6,7},{7,6},{8,9},{9,8},{10,11... | collective-permute-start | bytes 786440 | tf_op jit(solution)/shard_map/ppermute | solution.py:257

commit v7 on v5

--- a/solution.py
+++ b/solution.py
@@ -85,23 +85,26 @@
 def begin_kernel(*refs):
     inputs, (sent, pair_t, normed_t, mask_out, cols) = refs[:7], refs[7:12]
     local, (scr, gains, proj, sems) = refs[12:19], refs[19:]
-    parts = [(inputs[0].at[8 * n : 8 * n + 8], local[0].at[8 * n : 8 * n + 8]) for n in range(4)]
-    parts += [(inputs[2].at[0], local[2]), (inputs[1], local[1])] + list(zip(inputs[3:], local[3:]))
-    copies = [pltpu.make_async_copy(src, dst, sems.at[n]) for n, (src, dst) in enumerate(parts)]
+    early = [(inputs[0].at[8 * n : 8 * n + 8], local[0].at[8 * n : 8 * n + 8]) for n in range(4)]
+    early += list(zip(inputs[3:], local[3:]))
+    late = [(inputs[2].at[0], local[2]), (inputs[1], local[1])]
+    copies = [pltpu.make_async_copy(src, dst, sems.at[n]) for n, (src, dst) in enumerate(early + late)]
     for copy in copies:
         copy.start()
-    for copy in copies:
+    for copy in copies[: len(early)]:
         copy.wait()
     pair, mask, proj_w = local[:3]
     col = columns(local[3:], gains)
     cols[...] = col
+    for a in range(8):
+        block = jnp.concatenate([pair[8 * q + a] for q in range(4)], axis=0).astype(F32).T
+        pair_t[:, lanes_of(a)] = block.astype(BF16)
+        normed_t[:, lanes_of(a)] = norm_channels(block, col[:, 0:1], col[:, 2:3]).astype(BF16)
+    for copy in copies[len(early) :]:
+        copy.wait()
     m8 = first_mask(mask)
     mask_out[...] = m8
     w_t = transposed_halved(proj_w[...])
-    for a in range(8):
-        block = jnp.concatenate([pair[8 * q + a] for q in range(4)], axis=0).astype(F32).T
-        pair_t[:, lanes_of(a)] = block.astype(BF16)
-        normed_t[:, lanes_of(a)] = norm_channels(block, col[:, 0:1], col[:, 2:3]).astype(BF16)
     proj[...] = dot(w_t, normed_t[...], ((1,), (0,)))
     gated(proj, m8, scr)
     sent[...] = scr[0:2048, :].astype(BF16)

time: 112 us -> 112 us (level)
  no operation moved by 1% of the time
where the time goes in v7:
time: 112 us; the launch traced here: 111 us
  blocking collectives  102 us (91%)
  Pallas kernels  8.14 us (7%)
  waiting for transfers between devices  1.24 us (1%)
    all_to_all x4, blocking collectives, exchange(): return lax.all_to_all(v, CHIPS, 0, 0, tiled=True)  102 us
  transfers between devices with their start and end apart: 2, of which 2 were waited for; matrix products, arithmetic and copies ran while one was open for 0% of the time, Pallas kernels for 2%

profile of v7, /device:TPU:2, one launch (start us, length us, event | category | flops | bytes accessed | tf_op | source)
XLA Modules:
  0.0 111.4 jit_solution(1412008054224135481)
XLA Ops:
  0.0 2.1 %shard_map.91 = (bf16[2048,128]{1,0:T(8,128)(2,1)S(1)}, bf16[128,1024]{1,0:T(8,128)(2,1)S(1)}, bf16[128,1024]{1,0:T(8,128)(2,1)S(1)}, f32[8,128]{1,0:T(8,128)S(1)}, f32[128,8]{1,0:T(8,128)S(1)}) custom-call(bf16[32,32,128]{2,1,0:T(8,128)(2,1)} %refs_0_.1, s32[32,32]{1,0:T(8,128)} %refs_1_.1, bf16[2,128,512]{2,1,0:T(8,128)(2,1)} %proj_w.1, f32[2,128]{1,0:T(2,128)} %refs_3_.1, ...), custom_call_target="tpu_custom_call" | custom-call | tf_op jit(solution)/shard_map/pallas_call | solution.py:244
  2.1 34.6 %all_to_all.40 = bf16[128,16,128]{2,1,0:T(8,128)(2,1)S(1)} all-to-all(bf16[128,16,128]{2,1,0:T(8,128)(2,1)S(1)} %bitcast.18), channel_id=1, replica_groups=mesh['zh'=4,'x'=4,'zl'=2,'y'=4,'core'=2] {'zh','x','zl','y'}, dimensions={0} | all-to-all | bytes 1048576 | tf_op jit(solution)/shard_map/all_to_all | solution.py:238
  36.7 0.0 copy-start
  36.7 0.0 copy-start.1
  36.7 0.0 copy-start.2
  36.7 0.9 shard_map.92
  37.6 0.1 collective-permute-start
  37.7 0.0 copy-done
  37.7 0.0 copy-done.1
  37.7 0.0 copy-done.2
  37.7 1.0 shard_map.93
  38.7 0.5 collective-permute-done
  39.2 0.1 fusion
  39.2 21.0 %all_to_all.41 = bf16[128,8,128]{2,1,0:T(8,128)(2,1)S(1)} all-to-all(bf16[128,8,128]{2,1,0:T(8,128)(2,1)S(1)} %fusion), channel_id=1, replica_groups=mesh['zh'=4,'x'=4,'zl'=2,'y'=4,'core'=2] {'zh','x','zl','y'}, dimensions={0} | all-to-all | bytes 524288 | tf_op jit(solution)/shard_map/all_to_all | solution.py:238
  60.3 1.3 %shard_map.94 = (bf16[2048,128]{1,0:T(8,128)(2,1)S(1)}, bf16[128,1024]{1,0:T(8,128)(2,1)S(1)}, bf16[128,1024]{1,0:T(8,128)(2,1)S(1)}) custom-call(bf16[1024,128]{1,0:T(8,128)(2,1)S(1)} %bitcast.14, bf16[128,1024]{1,0:T(8,128)(2,1)S(1)} %get-tuple-element.28.pair_t, f32[128,1024]{1,0:T(8,128)S(1)} %get-tuple-element.29.gate, ...), custom_call_target="tpu_custom_call" | custom-call | tf_op jit(solution)/shard_map/pallas_call | solution.py:280
  61.6 25.1 %all_to_all.42 = bf16[128,16,128]{2,1,0:T(8,128)(2,1)S(1)} all-to-all(bf16[128,16,128]{2,1,0:T(8,128)(2,1)S(1)} %bitcast.17), channel_id=1, replica_groups=mesh['zh'=4,'x'=4,'zl'=2,'y'=4,'core'=2] {'zh','x','zl','y'}, dimensions={0} | all-to-all | bytes 1048576 | tf_op jit(solution)/shard_map/all_to_all | solution.py:238
  86.7 0.3 shard_map.95.lm
  87.0 0.1 collective-permute-start.1
  87.1 0.8 shard_map.96
  87.9 0.8 collective-permute-done.1.far
  88.6 0.5 shard_map.97
  89.1 21.0 %all_to_all.43 = bf16[128,8,128]{2,1,0:T(8,128)(2,1)S(1)} all-to-all(bf16[128,8,128]{2,1,0:T(8,128)(2,1)S(1)} %bitcast.16), channel_id=1, replica_groups=mesh['zh'=4,'x'=4,'zl'=2,'y'=4,'core'=2] {'zh','x','zl','y'}, dimensions={0} | all-to-all | bytes 524288 | tf_op jit(solution)/shard_map/all_to_all | solution.py:238
  110.1 1.3 %shard_map.98 = bf16[4,8,32,128]{3,2,1,0:T(8,128)(2,1)} custom-call(bf16[1024,128]{1,0:T(8,128)(2,1)S(1)} %bitcast.15, bf16[128,1024]{1,0:T(8,128)(2,1)S(1)} %get-tuple-element.38.state_t, f32[128,1024]{1,0:T(8,128)S(1)} %get-tuple-element.39.gate, f32[128,8]{1,0:T(8,128)S(1)} %get-tuple-element.31.cols, bf16[128,128]{1,0:T(8,128)(2,1)S(1)} %get-tuple-element.40.out_t), custom_call_target="tpu_custom_call" | custom-call | tf_op jit(solution)/shard_map/pallas_call | solution.py:295
Async XLA Ops:
  36.7 1.0 copy-start
  36.7 1.0 copy-start.1
  36.7 1.0 copy-start.2
  37.6 1.6 %collective-permute-start = (bf16[1024,128]{1,0:T(8,128)(2,1)S(1)}, bf16[1024,128]{1,0:T(8,128)(2,1)S(1)}, u32[]{:S(2)}, u32[]{:S(2)}) collective-permute-start(bf16[1024,128]{1,0:T(8,128)(2,1)S(1)} %get-tuple-element.27), channel_id=1, source_target_pairs={{0,1},{1,0},{2,3},{3,2},{4,5},{5,4},{6,7},{7,6},{8,9},{9,8},{10,11... | collective-permute-start | bytes 786440 | tf_op jit(solution)/shard_map/ppermute | solution.py:241
  87.0 1.6 %collective-permute-start.1 = (bf16[512,256]{1,0:T(8,128)(2,1)S(1)}, bf16[512,256]{1,0:T(8,128)(2,1)S(1)}, u32[]{:S(2)}, u32[]{:S(2)}) collective-permute-start(bf16[512,256]{1,0:T(8,128)(2,1)S(1)} %shard_map.95.lm), channel_id=1, source_target_pairs={{0,1},{1,0},{2,3},{3,2},{4,5},{5,4},{6,7},{7,6},{8,9},{9,8},{10,11... | collective-permute-start | bytes 786440 | tf_op jit(solution)/shard_map/ppermute | solution.py:241

commit v8 on v5

--- a/solution.py
+++ b/solution.py
@@ -83,18 +83,17 @@
 
 
 def begin_kernel(*refs):
-    inputs, (sent, pair_t, normed_t, mask_out, cols) = refs[:7], refs[7:12]
-    local, (scr, gains, proj, sems) = refs[12:19], refs[19:]
-    parts = [(inputs[0].at[8 * n : 8 * n + 8], local[0].at[8 * n : 8 * n + 8]) for n in range(4)]
-    parts += [(inputs[2].at[0], local[2]), (inputs[1], local[1])] + list(zip(inputs[3:], local[3:]))
-    copies = [pltpu.make_async_copy(src, dst, sems.at[n]) for n, (src, dst) in enumerate(parts)]
+    inputs, (sent, pair_t, normed_t, mask_out) = refs[:5], refs[5:9]
+    local, (scr, gains, proj, sems) = refs[9:14], refs[14:]
+    sources = (inputs[0], inputs[1], inputs[2].at[0], inputs[3], inputs[4])
+    copies = [pltpu.make_async_copy(src, dst, sems.at[n]) for n, (src, dst) in enumerate(zip(sources, local))]
     for copy in copies:
         copy.start()
     for copy in copies:
         copy.wait()
     pair, mask, proj_w = local[:3]
+    gains[...] = jnp.zeros_like(gains)
     col = columns(local[3:], gains)
-    cols[...] = col
     m8 = first_mask(mask)
     mask_out[...] = m8
     w_t = transposed_halved(proj_w[...])
@@ -185,7 +184,10 @@
     send[...] = outgoing_chunks(lm[...], rm, chunks).astype(BF16)
 
 
-def outgoing_keep_kernel(got, lm, normed_t, proj_w, gate_w, out_w, keep, gate, w_t, out_t, right, chunks):
+def outgoing_keep_kernel(
+    got, lm, normed_t, proj_w, gate_w, out_w, ig, ib, mg, mb, keep, gate, w_t, out_t, cols, right, chunks, gains
+):
+    cols[...] = columns((ig, ib, mg, mb), gains)
     keep[...] = outgoing_chunks(lm[...], outgoing_right(got, lax.axis_index("core"), right), chunks)
     gate[...] = sigmoid(dot(transposed(gate_w[0]), normed_t[...], ((1,), (0,))))
     w_t[...] = transposed_halved(proj_w[1])
@@ -237,23 +239,22 @@
     def swap(v):
         return lax.ppermute(v, "core", [(0, 1), (1, 0)])
 
-    first = (pair, mask, proj_w, ig, ib, mg, mb)
-    sent, pair_t, normed_t, m8, cols = pl.pallas_call(
+    first = (pair, mask, proj_w, ig, ib)
+    sent, pair_t, normed_t, m8 = pl.pallas_call(
         begin_kernel,
-        in_specs=[pl.BlockSpec(memory_space=pl.ANY)] * 7,
+        in_specs=[pl.BlockSpec(memory_space=pl.ANY)] * 5,
         out_shape=[
             jax.ShapeDtypeStruct((2048, 128), BF16),
             jax.ShapeDtypeStruct((128, 1024), BF16),
             jax.ShapeDtypeStruct((128, 1024), BF16),
             jax.ShapeDtypeStruct((8, 128), F32),
-            jax.ShapeDtypeStruct((128, 8), F32),
         ],
         scratch_shapes=[pltpu.VMEM(v.shape[1:] if v is proj_w else v.shape, v.dtype) for v in first]
         + [
             pltpu.VMEM(SCR, F32),
             pltpu.VMEM((8, 128), F32),
             pltpu.VMEM((512, 1024), F32),
-            pltpu.SemaphoreType.DMA((10,)),
+            pltpu.SemaphoreType.DMA((5,)),
         ],
         compiler_params=pltpu.CompilerParams(vmem_limit_bytes=VMEM_LIMIT),
     )(*(pltpu.with_memory_space_constraint(v, pltpu.HBM) for v in first))
@@ -267,12 +268,12 @@
         [(square, F32), (half, F32), ((16, 8, 8, 128), F32)],
     )(got)
     far = swap(send)
-    keep, gate, w_t, out_t = call(
+    keep, gate, w_t, out_t, cols = call(
         outgoing_keep_kernel,
-        [((1024, 128), F32), (wide, F32), ((512, 128), BF16), ((128, 128), BF16)],
-        [(half, F32), ((16, 8, 8, 128), F32)],
+        [((1024, 128), F32), (wide, F32), ((512, 128), BF16), ((128, 128), BF16), ((128, 8), F32)],
+        [(half, F32), ((16, 8, 8, 128), F32), ((8, 128), F32)],
         1 << 28,
-    )(got, lm, normed_t, proj_w, gate_w, out_w)
+    )(got, lm, normed_t, proj_w, gate_w, out_w, ig, ib, mg, mb)
     got = exchange((keep + far.astype(F32)).astype(BF16))
     sent, state_t, normed_t = call(
         middle_kernel,

time: 112 us -> 112 us (level)
  transfers between devices with their start and end apart: 2 -> 2, of which waited for: 2 -> 1; matrix products, arithmetic and copies ran while one was open for 0% -> 0% of each run, Pallas kernels for 2% -> 1%
where the time goes in v8:
time: 112 us
  blocking collectives  102 us (91%)
  Pallas kernels  7.89 us (7%)
    all_to_all x4, blocking collectives, exchange(): return lax.all_to_all(v, CHIPS, 0, 0, tiled=True)  102 us
  transfers between devices with their start and end apart: 2, of which 1 were waited for; matrix products, arithmetic and copies ran while one was open for 0% of the time, Pallas kernels for 1%

profile of v8, /device:TPU:2, one launch (start us, length us, event | category | flops | bytes accessed | tf_op | source)
XLA Modules:
  0.0 112.0 jit_solution(10865528441457315145)
XLA Ops:
  0.0 2.0 %shard_map.91 = (bf16[2048,128]{1,0:T(8,128)(2,1)S(1)}, bf16[128,1024]{1,0:T(8,128)(2,1)S(1)}, bf16[128,1024]{1,0:T(8,128)(2,1)S(1)}, f32[8,128]{1,0:T(8,128)S(1)}) custom-call(bf16[32,32,128]{2,1,0:T(8,128)(2,1)} %refs_0_.1, s32[32,32]{1,0:T(8,128)} %refs_1_.1, bf16[2,128,512]{2,1,0:T(8,128)(2,1)} %proj_w.1, f32[2,128]{1,0:T(2,128)} %ig.1, f32[2,128]{1,0:T(2,128)} %ib.1), custom_call_target="tpu_custom_call" | custom-call | tf_op jit(solution)/shard_map/pallas_call | solution.py:243
  2.0 34.6 %all_to_all.40 = bf16[128,16,128]{2,1,0:T(8,128)(2,1)S(1)} all-to-all(bf16[128,16,128]{2,1,0:T(8,128)(2,1)S(1)} %bitcast.18), channel_id=1, replica_groups=mesh['zh'=4,'x'=4,'zl'=2,'y'=4,'core'=2] {'zh','x','zl','y'}, dimensions={0} | all-to-all | bytes 1048576 | tf_op jit(solution)/shard_map/all_to_all | solution.py:237
  36.6 0.0 copy-start
  36.6 0.0 copy-start.1
  36.6 0.0 copy-start.2
  36.6 0.0 copy-start.4
  36.6 0.0 copy-start.5
  36.6 0.0 copy-start.6
  36.6 0.9 shard_map.92
  37.5 0.1 collective-permute-start
  37.6 0.0 copy-start.3
  37.6 0.0 copy-done
  37.6 0.0 copy-done.1
  37.6 0.0 copy-done.2
  37.6 0.0 copy-done.4
  37.6 0.0 copy-done.5
  37.6 0.0 copy-done.6
  37.6 0.6 copy-done.3
  38.2 0.9 shard_map.93
  39.1 0.0 collective-permute-done
  39.1 0.1 fusion
  39.2 21.4 %all_to_all.41 = bf16[128,8,128]{2,1,0:T(8,128)(2,1)S(1)} all-to-all(bf16[128,8,128]{2,1,0:T(8,128)(2,1)S(1)} %fusion), channel_id=1, replica_groups=mesh['zh'=4,'x'=4,'zl'=2,'y'=4,'core'=2] {'zh','x','zl','y'}, dimensions={0} | all-to-all | bytes 524288 | tf_op jit(solution)/shard_map/all_to_all | solution.py:237
  60.6 1.3 %shard_map.94 = (bf16[2048,128]{1,0:T(8,128)(2,1)S(1)}, bf16[128,1024]{1,0:T(8,128)(2,1)S(1)}, bf16[128,1024]{1,0:T(8,128)(2,1)S(1)}) custom-call(bf16[1024,128]{1,0:T(8,128)(2,1)S(1)} %bitcast.14, bf16[128,1024]{1,0:T(8,128)(2,1)S(1)} %get-tuple-element.28.pair_t, f32[128,1024]{1,0:T(8,128)S(1)} %get-tuple-element.29.gate, ...), custom_call_target="tpu_custom_call" | custom-call | tf_op jit(solution)/shard_map/pallas_call | solution.py:278
  61.9 25.3 %all_to_all.42 = bf16[128,16,128]{2,1,0:T(8,128)(2,1)S(1)} all-to-all(bf16[128,16,128]{2,1,0:T(8,128)(2,1)S(1)} %bitcast.17), channel_id=1, replica_groups=mesh['zh'=4,'x'=4,'zl'=2,'y'=4,'core'=2] {'zh','x','zl','y'}, dimensions={0} | all-to-all | bytes 1048576 | tf_op jit(solution)/shard_map/all_to_all | solution.py:237
  87.2 0.3 shard_map.95.lm
  87.6 0.1 collective-permute-start.1
  87.7 0.8 shard_map.96
  88.4 0.8 collective-permute-done.1.far
  89.2 0.5 shard_map.97
  89.6 21.0 %all_to_all.43 = bf16[128,8,128]{2,1,0:T(8,128)(2,1)S(1)} all-to-all(bf16[128,8,128]{2,1,0:T(8,128)(2,1)S(1)} %bitcast.16), channel_id=1, replica_groups=mesh['zh'=4,'x'=4,'zl'=2,'y'=4,'core'=2] {'zh','x','zl','y'}, dimensions={0} | all-to-all | bytes 524288 | tf_op jit(solution)/shard_map/all_to_all | solution.py:237
  110.7 1.3 %shard_map.98 = bf16[4,8,32,128]{3,2,1,0:T(8,128)(2,1)} custom-call(bf16[1024,128]{1,0:T(8,128)(2,1)S(1)} %bitcast.15, bf16[128,1024]{1,0:T(8,128)(2,1)S(1)} %get-tuple-element.38.state_t, f32[128,1024]{1,0:T(8,128)S(1)} %get-tuple-element.39.gate, f32[128,8]{1,0:T(8,128)S(1)} %get-tuple-element.31.cols, bf16[128,128]{1,0:T(8,128)(2,1)S(1)} %get-tuple-element.40.out_t), custom_call_target="tpu_custom_call" | custom-call | tf_op jit(solution)/shard_map/pallas_call | solution.py:293
Async XLA Ops:
  36.6 1.0 copy-start
  36.6 1.0 copy-start.1
  36.6 1.0 copy-start.2
  36.6 1.0 copy-start.4
  36.6 1.0 copy-start.5
  36.6 1.0 copy-start.6
  37.5 1.7 %collective-permute-start = (bf16[1024,128]{1,0:T(8,128)(2,1)S(1)}, bf16[1024,128]{1,0:T(8,128)(2,1)S(1)}, u32[]{:S(2)}, u32[]{:S(2)}) collective-permute-start(bf16[1024,128]{1,0:T(8,128)(2,1)S(1)} %get-tuple-element.27), channel_id=1, source_target_pairs={{0,1},{1,0},{2,3},{3,2},{4,5},{5,4},{6,7},{7,6},{8,9},{9,8},{10,11... | collective-permute-start | bytes 786440 | tf_op jit(solution)/shard_map/ppermute | solution.py:240
  37.6 0.7 copy-start.3
  87.6 1.6 %collective-permute-start.1 = (bf16[512,256]{1,0:T(8,128)(2,1)S(1)}, bf16[512,256]{1,0:T(8,128)(2,1)S(1)}, u32[]{:S(2)}, u32[]{:S(2)}) collective-permute-start(bf16[512,256]{1,0:T(8,128)(2,1)S(1)} %shard_map.95.lm), channel_id=1, source_target_pairs={{0,1},{1,0},{2,3},{3,2},{4,5},{5,4},{6,7},{7,6},{8,9},{9,8},{10,11... | collective-permute-start | bytes 786440 | tf_op jit(solution)/shard_map/ppermute | solution.py:240

commit v9 on v5

--- a/solution.py
+++ b/solution.py
@@ -130,7 +130,7 @@
     upd[...] = dot(out_t[...], tn[...], ((1,), (0,)))
     for a in range(8):
         lanes = lanes_of(a)
-        state = (pair_t[:, lanes].astype(F32) + gate[:, lanes] * upd[:, lanes]).astype(BF16)
+        state = (pair_t[:, lanes].astype(F32) + gate[:, lanes].astype(F32) * upd[:, lanes]).astype(BF16)
         state_out[:, lanes] = state
         normed_out[:, lanes] = norm_channels(state.astype(F32), col[:, 1:2], col[:, 3:4]).astype(BF16)
     proj[...] = dot(w_t[...], normed_out[...], ((1,), (0,)))
@@ -144,7 +144,7 @@
     upd[...] = dot(out_t[...], tn[...], ((1,), (0,)))
     for a in range(8):
         lanes = lanes_of(a)
-        state = (state_t[:, lanes].astype(F32) + gate[:, lanes] * upd[:, lanes]).T.astype(BF16)
+        state = (state_t[:, lanes].astype(F32) + gate[:, lanes].astype(F32) * upd[:, lanes]).T.astype(BF16)
         out[:, a] = state.reshape(4, 32, 128)
 
 
@@ -187,7 +187,7 @@
 
 def outgoing_keep_kernel(got, lm, normed_t, proj_w, gate_w, out_w, keep, gate, w_t, out_t, right, chunks):
     keep[...] = outgoing_chunks(lm[...], outgoing_right(got, lax.axis_index("core"), right), chunks)
-    gate[...] = sigmoid(dot(transposed(gate_w[0]), normed_t[...], ((1,), (0,))))
+    gate[...] = sigmoid(dot(transposed(gate_w[0]), normed_t[...], ((1,), (0,)))).astype(BF16)
     w_t[...] = transposed_halved(proj_w[1])
     out_t[...] = transposed(out_w[0])
 
@@ -205,7 +205,7 @@
         near[:, c] = t
 
     scatter_groups(dot(lm[...], rm[...], ((0,), (0,))), store)
-    gate[...] = sigmoid(dot(transposed(gate_w[1]), normed_t[...], ((1,), (0,))))
+    gate[...] = sigmoid(dot(transposed(gate_w[1]), normed_t[...], ((1,), (0,)))).astype(BF16)
     out_t[...] = transposed(out_w[1])
 
 
@@ -269,7 +269,7 @@
     far = swap(send)
     keep, gate, w_t, out_t = call(
         outgoing_keep_kernel,
-        [((1024, 128), F32), (wide, F32), ((512, 128), BF16), ((128, 128), BF16)],
+        [((1024, 128), F32), (wide, BF16), ((512, 128), BF16), ((128, 128), BF16)],
         [(half, F32), ((16, 8, 8, 128), F32)],
         1 << 28,
     )(got, lm, normed_t, proj_w, gate_w, out_w)
@@ -284,7 +284,7 @@
     far = swap(lm)
     near, rm, gate, out_t = call(
         incoming_near_kernel,
-        [((8, 8, 8, 128), F32), ((512, 256), BF16), (wide, F32), ((128, 128), BF16)],
+        [((8, 8, 8, 128), F32), ((512, 256), BF16), (wide, BF16), ((128, 128), BF16)],
         [(square, F32)],
         1 << 28,
     )(got, lm, normed_t, gate_w, out_w)

time: 112 us -> 112 us (level)
  transfers between devices with their start and end apart: 2 -> 2, of which waited for: 2 -> 2; matrix products, arithmetic and copies ran while one was open for 0% -> 0% of each run, Pallas kernels for 2% -> 1%
where the time goes in v9:
time: 112 us; the launch traced here: 111 us
  blocking collectives  102 us (91%)
  Pallas kernels  7.97 us (7%)
  waiting for transfers between devices  1.4 us (1%)
    all_to_all x4, blocking collectives, exchange(): return lax.all_to_all(v, CHIPS, 0, 0, tiled=True)  102 us
  transfers between devices with their start and end apart: 2, of which 2 were waited for; matrix products, arithmetic and copies ran while one was open for 0% of the time, Pallas kernels for 1%

profile of v9, /device:TPU:2, one launch (start us, length us, event | category | flops | bytes accessed | tf_op | source)
XLA Modules:
  0.0 111.4 jit_solution(1446279751546066357)
XLA Ops:
  0.0 2.1 %shard_map.91 = (bf16[2048,128]{1,0:T(8,128)(2,1)S(1)}, bf16[128,1024]{1,0:T(8,128)(2,1)S(1)}, bf16[128,1024]{1,0:T(8,128)(2,1)S(1)}, f32[8,128]{1,0:T(8,128)S(1)}, f32[128,8]{1,0:T(8,128)S(1)}) custom-call(bf16[32,32,128]{2,1,0:T(8,128)(2,1)} %refs_0_.1, s32[32,32]{1,0:T(8,128)} %refs_1_.1, bf16[2,128,512]{2,1,0:T(8,128)(2,1)} %proj_w.1, f32[2,128]{1,0:T(2,128)} %refs_3_.1, ...), custom_call_target="tpu_custom_call" | custom-call | tf_op jit(solution)/shard_map/pallas_call | solution.py:241
  2.1 34.6 %all_to_all.40 = bf16[128,16,128]{2,1,0:T(8,128)(2,1)S(1)} all-to-all(bf16[128,16,128]{2,1,0:T(8,128)(2,1)S(1)} %bitcast.18), channel_id=1, replica_groups=mesh['zh'=4,'x'=4,'zl'=2,'y'=4,'core'=2] {'zh','x','zl','y'}, dimensions={0} | all-to-all | bytes 1048576 | tf_op jit(solution)/shard_map/all_to_all | solution.py:235
  36.7 0.0 copy-start
  36.7 0.0 copy-start.1
  36.7 0.0 copy-start.2
  36.7 0.9 shard_map.92
  37.5 0.1 collective-permute-start
  37.6 0.0 copy-done
  37.6 0.0 copy-done.1
  37.6 0.0 copy-done.2
  37.7 0.8 shard_map.93
  38.5 0.6 collective-permute-done
  39.1 0.1 fusion
  39.2 21.0 %all_to_all.41 = bf16[128,8,128]{2,1,0:T(8,128)(2,1)S(1)} all-to-all(bf16[128,8,128]{2,1,0:T(8,128)(2,1)S(1)} %fusion), channel_id=1, replica_groups=mesh['zh'=4,'x'=4,'zl'=2,'y'=4,'core'=2] {'zh','x','zl','y'}, dimensions={0} | all-to-all | bytes 524288 | tf_op jit(solution)/shard_map/all_to_all | solution.py:235
  60.2 1.4 %shard_map.94 = (bf16[2048,128]{1,0:T(8,128)(2,1)S(1)}, bf16[128,1024]{1,0:T(8,128)(2,1)S(1)}, bf16[128,1024]{1,0:T(8,128)(2,1)S(1)}) custom-call(bf16[1024,128]{1,0:T(8,128)(2,1)S(1)} %bitcast.14, bf16[128,1024]{1,0:T(8,128)(2,1)S(1)} %get-tuple-element.28.pair_t, bf16[128,1024]{1,0:T(8,128)(2,1)S(1)} %get-tuple-element.29.gate, ...), custom_call_target="tpu_custom_call" | custom-call | tf_op jit(solution)/shard_map/pallas_call | solution.py:277
  61.6 25.1 %all_to_all.42 = bf16[128,16,128]{2,1,0:T(8,128)(2,1)S(1)} all-to-all(bf16[128,16,128]{2,1,0:T(8,128)(2,1)S(1)} %bitcast.17), channel_id=1, replica_groups=mesh['zh'=4,'x'=4,'zl'=2,'y'=4,'core'=2] {'zh','x','zl','y'}, dimensions={0} | all-to-all | bytes 1048576 | tf_op jit(solution)/shard_map/all_to_all | solution.py:235
  86.7 0.3 shard_map.95.lm
  87.0 0.1 collective-permute-start.1
  87.1 0.8 shard_map.96
  87.8 0.8 collective-permute-done.1.far
  88.6 0.5 shard_map.97
  89.1 21.0 %all_to_all.43 = bf16[128,8,128]{2,1,0:T(8,128)(2,1)S(1)} all-to-all(bf16[128,8,128]{2,1,0:T(8,128)(2,1)S(1)} %bitcast.16), channel_id=1, replica_groups=mesh['zh'=4,'x'=4,'zl'=2,'y'=4,'core'=2] {'zh','x','zl','y'}, dimensions={0} | all-to-all | bytes 524288 | tf_op jit(solution)/shard_map/all_to_all | solution.py:235
  110.1 1.3 %shard_map.98 = bf16[4,8,32,128]{3,2,1,0:T(8,128)(2,1)} custom-call(bf16[1024,128]{1,0:T(8,128)(2,1)S(1)} %bitcast.15, bf16[128,1024]{1,0:T(8,128)(2,1)S(1)} %get-tuple-element.38.state_t, bf16[128,1024]{1,0:T(8,128)(2,1)S(1)} %get-tuple-element.39.gate, f32[128,8]{1,0:T(8,128)S(1)} %get-tuple-element.31.cols, bf16[128,128]{1,0:T(8,128)(2,1)S(1)} %get-tuple-element.40.out_t), custom_call_target="tpu_custom_call" | custom-call | tf_op jit(solution)/shard_map/pallas_call | solution.py:292
Async XLA Ops:
  36.7 1.0 copy-start
  36.7 1.0 copy-start.1
  36.7 1.0 copy-start.2
  37.5 1.6 %collective-permute-start = (bf16[1024,128]{1,0:T(8,128)(2,1)S(1)}, bf16[1024,128]{1,0:T(8,128)(2,1)S(1)}, u32[]{:S(2)}, u32[]{:S(2)}) collective-permute-start(bf16[1024,128]{1,0:T(8,128)(2,1)S(1)} %get-tuple-element.27), channel_id=1, source_target_pairs={{0,1},{1,0},{2,3},{3,2},{4,5},{5,4},{6,7},{7,6},{8,9},{9,8},{10,11... | collective-permute-start | bytes 786440 | tf_op jit(solution)/shard_map/ppermute | solution.py:238
  87.0 1.6 %collective-permute-start.1 = (bf16[512,256]{1,0:T(8,128)(2,1)S(1)}, bf16[512,256]{1,0:T(8,128)(2,1)S(1)}, u32[]{:S(2)}, u32[]{:S(2)}) collective-permute-start(bf16[512,256]{1,0:T(8,128)(2,1)S(1)} %shard_map.95.lm), channel_id=1, source_target_pairs={{0,1},{1,0},{2,3},{3,2},{4,5},{5,4},{6,7},{7,6},{8,9},{9,8},{10,11... | collective-permute-start | bytes 786440 | tf_op jit(solution)/shard_map/ppermute | solution.py:238
